TPU v7x, 256 devices: a whole 4x4x8 slice. The times are simulated.
256 devices in a mesh: dom: 32 (over z, y), rep: 8 (over x, core).
Axes of the slice: x: 4, y: 4, z: 8, core: 2. Of those that a mesh axis runs over, the one named last changes fastest.
Arguments:
- features: bfloat16 [8, 128, 64, 256], P('rep', 'dom'), may hold values from -6 to 6
- coords: int32 [8, 3, 8192], P('rep', None, 'dom'), may hold values from 0 to 47
- kernel_points: float32 [15, 3], replicated, may hold values from -1.2 to 1.2
- weights: bfloat16 [3840, 256], replicated, may hold values from -0.09375 to 0.09375
- support_slot: int32 [8, 128, 4], P('rep', 'dom'), may hold values from 0 to 13, as said below
- slot_mask: int32 [8, 128, 4, 64, 64], P('rep', 'dom'), may hold values 0 or 1
- send_leaf: int32 [8, 32, 5, 2], P('rep', 'dom'), may hold values from 0 to 3
- cotangent: bfloat16 [8, 128, 64, 256], P('rep', 'dom'), may hold values from -6 to 6
Outputs:
- output: bfloat16 [8, 128, 64, 256], P('rep', 'dom')
- grad_features: bfloat16 [8, 128, 64, 256], P('rep', 'dom')
- grad_weight: float32 [3840, 256], replicated
Inputs may be any that keep to these rules, and one draw needn't show every extreme that they name: `support_slot`: entries below 4 name the device's own leaves; entry 4 + b * 2 + t names the t-th leaf offered by the partner at bit b, and every such entry is named by some slot of the device; slot 0 of each query leaf names the leaf itself.
All inputs are finite; a program needn't handle non-finite values. No bound on the sum of `slot_mask` on one device may be relied on, other than what follows from the above.
Results may differ from a plain program's by a relative error of at most 0.0057.
Values may be sent and summed in bfloat16 or wider, within the bound.
A program may use at most 64 MiB of HBM per device.

v0:
```python
import jax
import jax.numpy as jnp
from jax import lax
from jax.sharding import PartitionSpec as P

QUANT = 0.0625
EPSILON = 1e-06


def swapped(block, axis, stride):
    count = lax.axis_size(axis)
    route = []
    for low in range(count):
        high = low | 1 << stride
        if high != low and high < count:
            route += [(low, high), (high, low)]
    return lax.ppermute(block, axis, route)


def correlation(query_pos, support_pos, slot_masks, kernel_points):
    squared = jnp.zeros(
        (query_pos.shape[1], kernel_points.shape[0], query_pos.shape[2], support_pos.shape[2]),
        jnp.float32,
    )
    for component in range(3):
        difference = (
            support_pos[component][:, None, None, :]
            - query_pos[component][:, None, :, None]
            - kernel_points[:, component][None, :, None, None]
        )
        squared = squared + difference * difference
    distance = jnp.sqrt(squared + EPSILON)
    weight_map = jnp.maximum(1.0 - distance, 0.0) * slot_masks.astype(jnp.float32)[:, None, :, :]
    return weight_map.astype(jnp.bfloat16)


def shards(features, coords, kernel_points, weights, support_slot, slot_mask, send_leaf, cotangent):
    leaf_feats = features[0]
    leaf_count, points, channels = leaf_feats.shape
    kernels = kernel_points.shape[0]
    positions = (coords[0].astype(jnp.float32) * QUANT).reshape(3, leaf_count, points)
    rounds = lax.axis_size("dom").bit_length() - 1
    send_table = send_leaf[0, 0]
    bound_count = send_table.shape[1]
    send_feats = leaf_feats[send_table]
    send_pos = positions[:, send_table].astype(jnp.bfloat16)
    got_feats = []
    got_pos = []
    all_feats, all_pos = (
        lax.all_gather(send_feats[None], "dom", axis=0, tiled=True),
        lax.all_gather(send_pos[None], "dom", axis=0, tiled=True),
    )
    own_index = lax.axis_index("dom")
    for bit_index in range(rounds):
        partner = jnp.bitwise_xor(own_index, 1 << bit_index)
        got_feats.append(lax.dynamic_index_in_dim(all_feats, partner, 0, keepdims=False)[bit_index])
        got_pos.append(lax.dynamic_index_in_dim(all_pos, partner, 0, keepdims=False)[:, bit_index])
    pool_feats = jnp.concatenate([leaf_feats] + got_feats, 0)
    pool_pos = jnp.concatenate([positions] + [piece.astype(jnp.float32) for piece in got_pos], 1)
    slot_table = support_slot[0]
    near_count = slot_table.shape[1]
    support_feats = pool_feats[slot_table]
    pieces = []
    for slot_index in range(near_count):
        pieces.append(
            correlation(
                positions,
                pool_pos[:, slot_table[:, slot_index]],
                slot_mask[0][:, slot_index],
                kernel_points,
            )
        )
    correlated = jnp.stack(pieces, 1)
    summed = jnp.einsum(
        "lnkij,lnjc->lkic", correlated, support_feats, preferred_element_type=jnp.float32
    )
    summed_low = summed.astype(jnp.bfloat16)
    weight_cube = weights.reshape(kernels, channels, -1)
    output = jnp.einsum(
        "lkic,kco->lio", summed_low, weight_cube, preferred_element_type=jnp.float32
    ).astype(jnp.bfloat16)
    upstream = cotangent[0]
    grad_summed = jnp.einsum(
        "lio,kco->lkic", upstream, weight_cube, preferred_element_type=jnp.float32
    ).astype(jnp.bfloat16)
    grad_local = jnp.einsum(
        "lkic,lio->kco", summed_low, upstream, preferred_element_type=jnp.float32
    )
    devices = lax.axis_size("dom") * lax.axis_size("rep")
    grad_flat = grad_local.reshape(kernels * channels, -1)
    grad_weight = lax.psum(grad_flat, ("dom", "rep")) / devices
    grad_support = jnp.einsum(
        "lnkij,lkic->lnjc", correlated, grad_summed, preferred_element_type=jnp.float32
    )
    pool_size = leaf_count + rounds * bound_count
    selector = (
        jnp.arange(pool_size, dtype=jnp.int32)[:, None] == slot_table.reshape(-1)[None, :]
    ).astype(jnp.float32)
    grad_pool = jnp.dot(
        selector,
        grad_support.reshape(leaf_count * near_count, points * channels),
        precision=lax.Precision.HIGHEST,
        preferred_element_type=jnp.float32,
    )
    grad_pool = grad_pool.reshape(pool_size, points, channels)
    grad_leaves = grad_pool[:leaf_count]
    for bit_index in range(rounds):
        offset = leaf_count + bit_index * bound_count
        returned = swapped(grad_pool[offset : offset + bound_count], "dom", bit_index)
        back_select = (
            jnp.arange(leaf_count, dtype=jnp.int32)[:, None] == send_table[bit_index][None, :]
        ).astype(jnp.float32)
        grad_leaves = grad_leaves + jnp.dot(
            back_select,
            returned.reshape(bound_count, -1),
            precision=lax.Precision.HIGHEST,
            preferred_element_type=jnp.float32,
        ).reshape(leaf_count, points, channels)
    return (output[None], grad_leaves.astype(jnp.bfloat16)[None], grad_weight)


def solution(mesh):
    in_specs = (
        P("rep", "dom", None, None),
        P("rep", None, "dom"),
        P(),
        P(),
        P("rep", "dom", None),
        P("rep", "dom", None, None, None),
        P("rep", "dom", None, None),
        P("rep", "dom", None, None),
    )
    out_specs = (P("rep", "dom", None, None), P("rep", "dom", None, None), P())
    return jax.shard_map(shards, mesh=mesh, in_specs=in_specs, out_specs=out_specs, check_vma=False)
```

profile of v0, /device:TPU:1, one launch (start us, length us, event | category | flops | bytes accessed | tf_op | source)
XLA Modules:
  0.0 411.7 jit_solution(7925493637978580155)
XLA Ops:
  7.2 0.9 compare_select_fusion.5
  8.3 2.2 gather_fusion.5
  10.6 0.8 eq.91
  11.4 0.7 compare_select_fusion
  12.2 0.7 convert_multiply_fusion
  13.1 0.6 gather_fusion
  13.7 43.3 %all-gather = bf16[96,5,2,64]{3,2,1,0:T(2,128)(2,1)S(1)} all-gather(bf16[3,5,2,64]{3,2,1,0:T(2,128)(2,1)S(1)} %bitcast.267), channel_id=2, replica_groups=mesh['dom'=32,'rep'=8] {'dom'}, dimensions={0}, use_global_device_ids=true | all-gather | bytes 126720 | tf_op jit(solution)/shard_map/all_gather | solution.py:51
  57.0 1.0 fusion.23
  58.1 0.6 gather_fusion.1
  58.7 0.6 gather_fusion.2
  59.3 0.6 gather_fusion.3
  59.9 0.6 gather_fusion.4
  60.6 0.8 slice_bitcast_fusion.7
  61.5 0.1 broadcast_subtract_fusion.9
  61.6 0.1 broadcast_subtract_fusion.10
  61.9 7.2 %multiply_convert_fusion.3 = (bf16[4,1,15,64,64]{4,3,1,2,0:T(8,128)(2,1)}, bf16[4,1,15,64,64]{4,3,1,2,0:T(8,128)(2,1)}, bf16[4,1,15,64,64]{4,3,1,2,0:T(8,128)(2,1)}, bf16[4,1,15,64,64]{4,3,1,2,0:T(8,128)(2,1)}) fusion(f32[4,64,64]{2,1,0:T(8,128)S(1)} %get-tuple-element.32, f32[15]{0:T(128)S(1)} %get-tuple-element.68, f32[4,64,64]{2,1,0:T(8,128)S(1)} %get-tuple-element.63, ...), kind=kLoop, calls=%fused_computation.18 | loop fusion | flops 12779520 | bytes 3014836 | tf_op jit(solution)/shard_map/convert_element_type | solution.py:34
  69.1 4.0 fusion
  73.1 0.6 copy.62
  73.7 0.3 copy-done.3
  74.0 0.6 fusion.21
  74.6 48.5 %all-gather.4.cloned.1.call-done = bf16[160,2,64,256]{3,2,1,0:T(8,128)(2,1)} async-done(((bf16[5,2,64,256]{3,2,1,0:T(8,128)(2,1)}), bf16[160,2,64,256]{3,2,1,0:T(8,128)(2,1)}) %all-gather.4.cloned.1.call-update) | async-done | bytes 10485776 | tf_op jit(solution)/shard_map/all_gather | solution.py:50
  123.1 0.8 fusion.20
  124.0 0.8 fusion.19
  124.8 0.8 fusion.18
  125.7 0.8 fusion.17
  126.5 0.8 fusion.16
  127.4 1.4 gather_fusion.6
  128.7 4.0 bitcast_convert_fusion
  132.8 0.1 copy.61
  132.9 1.1 copy-done.1
  134.0 2.6 convolution_bitcast_fusion
  136.7 0.2 fusion.50
  137.0 0.2 collective-permute-start
  137.2 2.1 collective-permute-start.1
  139.4 3.1 collective-permute-start.3
  142.5 1.5 collective-permute-start.4
  144.0 0.3 slice_reduce_fusion.3
  144.2 0.5 convolution_add_fusion.4
  144.8 0.5 convolution_add_fusion.3
  145.3 0.5 convolution_add_fusion.2
  145.9 0.1 collective-permute-done.3
  146.0 0.5 convolution_add_fusion.1
  146.5 5.6 %collective-permute-done.4 = f32[2,64,256]{2,1,0:T(8,128)S(1)} collective-permute-done((f32[2,64,256]{2,1,0:T(8,128)S(1)}, f32[2,64,256]{2,1,0:T(8,128)S(1)}, u32[]{:S(2)}, u32[]{:S(2)}) %collective-permute-start.4) | collective-permute-done | bytes 131104 | tf_op jit(solution)/shard_map/ppermute | solution.py:17
  152.1 0.5 fusion.7
  152.7 0.7 copy.51
  153.4 1.3 fusion.8
  154.7 245.9 %all-reduce.2.cloned.1.call-done = f32[3840,256]{1,0:T(8,128)} async-done(((f32[3840,256]{1,0:T(8,128)}), f32[3840,256]{1,0:T(8,128)}) %all-reduce.2.cloned.1.call-update) | async-done | bytes 3932176 | tf_op jit(solution)/shard_map/psum | solution.py:91
  400.6 4.3 %broadcast_multiply_fusion = f32[3840,256]{1,0:T(8,128)} fusion(f32[3840,256]{1,0:T(8,128)} %all-reduce.2.cloned.1.call-done), kind=kLoop, calls=%fused_computation.12 | loop fusion | flops 983040 | bytes 7864320 | tf_op jit(solution)/shard_map/div | solution.py:91
  (59 shorter events, 1.3 us)
Async XLA Ops:
  7.2 61.9 %copy-start = (bf16[3840,256]{1,0:T(8,128)(2,1)S(1)}, bf16[3840,256]{1,0:T(8,128)(2,1)}, u32[]{:S(2)}) copy-start(bf16[3840,256]{1,0:T(8,128)(2,1)} %param.11) | copy-start | bytes 5898244
  7.2 54.6 %copy-start.4 = (s32[1,4,4,64,64]{4,3,2,1,0:T(8,128)S(1)}, s32[1,4,4,64,64]{4,3,2,1,0:T(8,128)}, u32[]{:S(2)}) copy-start(s32[1,4,4,64,64]{4,3,2,1,0:T(8,128)} %param.13) | copy-start | bytes 786436
  7.2 115.9 %all-gather.4.cloned.1.call-start = ((), (), s32[]{:S(2)}) async-start(), calls=%async_computation.1 | async-start | bytes 10813440 | tf_op jit(solution)/shard_map/all_gather | solution.py:50
  10.5 390.0 %all-reduce.2.cloned.1.call-start = ((), (), s32[]{:S(2)}) async-start(), calls=%async_computation | async-start | bytes 7864320 | tf_op jit(solution)/shard_map/psum | solution.py:91
  61.9 7.2 %copy-start.6 = (bf16[1,4,64,256]{3,2,1,0:T(8,128)(2,1)S(1)}, bf16[1,4,64,256]{3,2,1,0:T(8,128)(2,1)}, u32[]{:S(2)}) copy-start(bf16[1,4,64,256]{3,2,1,0:T(8,128)(2,1)} %param.15) | copy-start | bytes 393220
  73.1 0.9 copy-start.3
  132.7 1.3 copy-start.1
  132.7 1.3 copy-start.7
  136.7 7.3 %copy-start.5 = (s32[1,1,5,2]{2,3,1,0:T(2,128)S(1)}, s32[1,1,5,2]{2,3,1,0:T(2,128)}, u32[]{:S(2)}) copy-start(s32[1,1,5,2]{2,3,1,0:T(2,128)} %param.14) | copy-start | bytes 124
  137.0 7.3 %collective-permute-start = (f32[2,64,256]{2,1,0:T(8,128)S(1)}, f32[2,64,256]{2,1,0:T(8,128)S(1)}, u32[]{:S(2)}, u32[]{:S(2)}) collective-permute-start(f32[2,64,256]{2,1,0:T(8,128)S(1)} %bitcast.260), channel_id=1, source_target_pairs={{0,8},{8,0},{16,24},{24,16},{32,40},{40,32},{48,56},{56,48},{64,72... | collective-permute-start | bytes 393224 | tf_op jit(solution)/shard_map/ppermute | solution.py:17
  137.2 7.6 %collective-permute-start.1 = (f32[2,64,256]{2,1,0:T(8,128)S(1)}, f32[2,64,256]{2,1,0:T(8,128)S(1)}, u32[]{:S(2)}, u32[]{:S(2)}) collective-permute-start(f32[2,64,256]{2,1,0:T(8,128)S(1)} %bitcast.259), channel_id=1, source_target_pairs={{0,16},{16,0},{8,24},{24,8},{32,48},{48,32},{40,56},{56,40},{64,80... | collective-permute-start | bytes 393224 | tf_op jit(solution)/shard_map/ppermute | solution.py:17
  139.3 6.0 %collective-permute-start.2 = (f32[2,64,256]{2,1,0:T(8,128)S(1)}, f32[2,64,256]{2,1,0:T(8,128)S(1)}, u32[]{:S(2)}, u32[]{:S(2)}) collective-permute-start(f32[2,64,256]{2,1,0:T(8,128)S(1)} %bitcast.258), channel_id=1, source_target_pairs={{0,32},{32,0},{8,40},{40,8},{16,48},{48,16},{24,56},{56,24},{64,96... | collective-permute-start | bytes 393224 | tf_op jit(solution)/shard_map/ppermute | solution.py:17
  139.4 6.6 %collective-permute-start.3 = (f32[2,64,256]{2,1,0:T(8,128)S(1)}, f32[2,64,256]{2,1,0:T(8,128)S(1)}, u32[]{:S(2)}, u32[]{:S(2)}) collective-permute-start(f32[2,64,256]{2,1,0:T(8,128)S(1)} %bitcast.257), channel_id=1, source_target_pairs={{0,64},{64,0},{8,72},{72,8},{16,80},{80,16},{24,88},{88,24},{32,96... | collective-permute-start | bytes 393224 | tf_op jit(solution)/shard_map/ppermute | solution.py:17
  142.5 10.9 %copy-start.2 = (bf16[4,15,64,256]{3,2,1,0:T(8,128)(2,1)S(1)}, bf16[4,15,64,256]{3,2,1,0:T(8,128)(2,1)}, u32[]{:S(2)}) copy-start(bf16[4,15,64,256]{3,2,1,0:T(8,128)(2,1)} %copy-done.1) | copy-start | bytes 5898244
  142.5 9.7 %collective-permute-start.4 = (f32[2,64,256]{2,1,0:T(8,128)S(1)}, f32[2,64,256]{2,1,0:T(8,128)S(1)}, u32[]{:S(2)}, u32[]{:S(2)}) collective-permute-start(f32[2,64,256]{2,1,0:T(8,128)S(1)} %bitcast.256), channel_id=1, source_target_pairs={{0,128},{128,0},{8,136},{136,8},{16,144},{144,16},{24,152},{152,24... | collective-permute-start | bytes 393224 | tf_op jit(solution)/shard_map/ppermute | solution.py:17
Sparse Core Ops, SparseCore 0:
  10.7 112.4 all-gather.3
  136.8 263.7 all-reduce.1
where the time goes:
time: 413 us; the launch traced here: 412 us
  waiting for transfers between devices  300 us (73%)
  blocking collectives  43.3 us (10%)
  local copies, waits for them, and re-layouts  16.4 us (4%)
  other arithmetic  15.2 us (4%)
  matrix products  15.2 us (4%)
  between operations  14.5 us (4%)
  starting transfers between devices  6.95 us (2%)
    psum x1, waiting for transfers between devices, shards(): grad_weight = lax.psum(grad_flat, ('dom', 'rep')) / devices  246 us
    all_gather x1, waiting for transfers between devices, shards(): lax.all_gather(send_feats[None], 'dom', axis=0, tiled=True)  48.5 us
    all_gather x1, blocking collectives, shards(): lax.all_gather(send_pos[None], 'dom', axis=0, tiled=True)  43.3 us
  transfers between devices with their start and end apart: 7, of which 4 were waited for; matrix products, arithmetic and copies ran while one was open for 6% of the time, Pallas kernels for 0%

commit v1 on v0

--- a/solution.py
+++ b/solution.py
@@ -1,10 +1,17 @@
+import functools
+
 import jax
 import jax.numpy as jnp
 from jax import lax
+from jax.experimental import pallas as pl
+from jax.experimental.pallas import tpu as pltpu
 from jax.sharding import PartitionSpec as P
 
 QUANT = 0.0625
 EPSILON = 1e-06
+CORES = 2
+NY = 4
+MESH = pl.DeviceIdType.MESH
 
 
 def swapped(block, axis, stride):
@@ -15,6 +22,202 @@
         if high != low and high < count:
             route += [(low, high), (high, low)]
     return lax.ppermute(block, axis, route)
+
+
+def place():
+    dom, rep = lax.axis_index("dom"), lax.axis_index("rep")
+    return rep // CORES, lax.rem(dom, NY), dom // NY, lax.rem(rep, CORES)
+
+
+def device(x, y, z, core):
+    return (z * NY + y, x * CORES + core)
+
+
+def greet(others):
+    barrier = pltpu.get_barrier_semaphore()
+    for other in others:
+        pl.semaphore_signal(barrier, inc=1, device_id=other, device_id_type=MESH)
+    pl.semaphore_wait(barrier, len(others))
+
+
+def remote(src, dst, send, recv, other):
+    copy = pltpu.make_async_remote_copy(
+        src_ref=src, dst_ref=dst, send_sem=send, recv_sem=recv, device_id=other, device_id_type=MESH
+    )
+    copy.start()
+    return copy
+
+
+def around(position, count):
+    return [lax.rem(position + step, count) for step in range(1, count)]
+
+
+def sum_kernel(nx, nz, kernels, p, final, mine, got0, got_first, part, got_second, slab, got_z, piece, gather_z, gather_second, send, recv):
+    x, y, z, core = place()
+    sibling = device(x, y, z, 1 - core)
+    lanes = {"x": (x, nx, lambda o: device(o, y, z, core)), "y": (y, NY, lambda o: device(x, o, z, core))}
+    z_ring = [(o, device(x, y, o, core)) for o in around(z, nz)]
+    others = [sibling] + [d for _, d in z_ring]
+    for at, count, to in lanes.values():
+        others += [to(o) for o in around(at, count)]
+    greet(others)
+
+    rows = p.shape[2]
+    per_z = gather_z.shape[0] // nz
+    half = (kernels + 1) // 2
+    groups = [(0, half, "x", "y"), (half, kernels - half, "y", "x")]
+    number = [0]
+
+    def push(src, dst, other):
+        index = number[0]
+        number[0] += 1
+        return remote(src, dst, send.at[index], recv.at[index], other)
+
+    started = []
+
+    def wait_all(copies):
+        for copy in copies:
+            copy.wait_recv()
+        started.extend(copies)
+
+    copies = []
+    for k0, nk, _, _ in groups:
+        copies.append([push(p.at[1 - core, pl.ds(k0, nk)], got0.at[pl.ds(k0, nk)], sibling)])
+    firsts = []
+    for (k0, nk, first, _), copy in zip(groups, copies):
+        wait_all(copy)
+
+        def add0(k, _):
+            total = p[core, k].astype(jnp.float32) + got0[k].astype(jnp.float32)
+            mine[k] = total.astype(jnp.bfloat16)
+            return 0
+
+        lax.fori_loop(k0, k0 + nk, add0, 0)
+        at, count, to = lanes[first]
+        block = rows // count
+        firsts.append([
+            push(
+                mine.at[pl.ds(k0, nk), pl.ds(pl.multiple_of(o * block, block), block)],
+                got_first.at[step, pl.ds(k0, nk)],
+                to(o),
+            )
+            for step, o in enumerate(around(at, count))
+        ])
+    seconds = []
+    for (k0, nk, first, second), copy in zip(groups, firsts):
+        wait_all(copy)
+        at, count, _ = lanes[first]
+        block = rows // count
+        own = pl.ds(pl.multiple_of(at * block, block), block)
+
+        def add1(k, _):
+            total = mine[k, own].astype(jnp.float32)
+            for step in range(count - 1):
+                total = total + got_first[step, k].astype(jnp.float32)
+            part[k] = total.astype(jnp.bfloat16)
+            return 0
+
+        lax.fori_loop(k0, k0 + nk, add1, 0)
+        at, count, to = lanes[second]
+        block = part.shape[1] // count
+        seconds.append([
+            push(
+                part.at[pl.ds(k0, nk), pl.ds(pl.multiple_of(o * block, block), block)],
+                got_second.at[step, pl.ds(k0, nk)],
+                to(o),
+            )
+            for step, o in enumerate(around(at, count))
+        ])
+    for k in range(kernels, slab.shape[0]):
+        slab[k] = jnp.zeros(slab.shape[1:], slab.dtype)
+    for (k0, nk, _, second), copy in zip(groups, seconds):
+        wait_all(copy)
+        at, count, _ = lanes[second]
+        block = part.shape[1] // count
+        own = pl.ds(pl.multiple_of(at * block, block), block)
+
+        def add2(k, _):
+            total = part[k, own].astype(jnp.float32)
+            for step in range(count - 1):
+                total = total + got_second[step, k].astype(jnp.float32)
+            slab[k] = total.astype(jnp.bfloat16)
+            return 0
+
+        lax.fori_loop(k0, k0 + nk, add2, 0)
+    wait_all([])
+    copies = [
+        push(slab.at[pl.ds(o * per_z, per_z)], got_z.at[step], other) for step, (o, other) in enumerate(z_ring)
+    ]
+    wait_all(copies)
+    own_z = pl.ds(z * per_z, per_z)
+    total = slab[own_z].astype(jnp.float32)
+    for step in range(nz - 1):
+        total = total + got_z[step].astype(jnp.float32)
+    devices = nx * NY * nz * CORES
+    piece[...] = (total / devices).astype(jnp.bfloat16)
+    copies = [push(piece, gather_z.at[own_z], other) for _, other in z_ring]
+    gather_z[own_z] = piece[...]
+    wait_all(copies)
+    backs = []
+    for k0, nk, _, second in groups:
+        at, count, to = lanes[second]
+        block = part.shape[1] // count
+        own = pl.ds(pl.multiple_of(at * block, block), block)
+        backs.append([
+            push(gather_z.at[pl.ds(k0, nk)], gather_second.at[pl.ds(k0, nk), own], to(o)) for o in around(at, count)
+        ])
+        gather_second[pl.ds(k0, nk), own] = gather_z[pl.ds(k0, nk)]
+    fronts = []
+    for (k0, nk, first, _), copy in zip(groups, backs):
+        wait_all(copy)
+        at, count, to = lanes[first]
+        block = rows // count
+        own = pl.ds(pl.multiple_of(at * block, block), block)
+        fronts.append([
+            push(gather_second.at[pl.ds(k0, nk)], final.at[core, pl.ds(k0, nk), own], to(o)) for o in around(at, count)
+        ])
+        final[core, pl.ds(k0, nk), own] = gather_second[pl.ds(k0, nk)]
+    lasts = []
+    for (k0, nk, _, _), copy in zip(groups, fronts):
+        wait_all(copy)
+        half_ref = final.at[core, pl.ds(k0, nk)]
+        lasts.append(push(half_ref, half_ref, sibling))
+    wait_all(lasts)
+    for copy in started:
+        copy.wait_send()
+
+
+def summed_weights(partial, nx, nz):
+    _, kernels, rows, lanes = partial.shape
+    per_z = -(-kernels // nz)
+    bf16 = jnp.bfloat16
+    wide = max(nx, NY)
+    copies = 2 * (1 + (nx - 1) + (NY - 1)) * 2 + 2 * (nz - 1)
+    narrow = min(nx, NY)
+    return pl.pallas_call(
+        functools.partial(sum_kernel, nx, nz, kernels),
+        out_shape=jax.ShapeDtypeStruct(partial.shape, bf16),
+        in_specs=[pl.BlockSpec(memory_space=pltpu.VMEM)],
+        out_specs=pl.BlockSpec(memory_space=pltpu.VMEM),
+        scratch_shapes=[
+            pltpu.VMEM((kernels, rows, lanes), bf16),
+            pltpu.VMEM((kernels, rows, lanes), bf16),
+            pltpu.VMEM((wide - 1, kernels, rows // narrow, lanes), bf16),
+            pltpu.VMEM((kernels, rows // narrow, lanes), bf16),
+            pltpu.VMEM((wide - 1, kernels, rows // (nx * NY), lanes), bf16),
+            pltpu.VMEM((per_z * nz, rows // (nx * NY), lanes), bf16),
+            pltpu.VMEM((nz - 1, per_z, rows // (nx * NY), lanes), bf16),
+            pltpu.VMEM((per_z, rows // (nx * NY), lanes), bf16),
+            pltpu.VMEM((per_z * nz, rows // (nx * NY), lanes), bf16),
+            pltpu.VMEM((kernels, rows // narrow, lanes), bf16),
+            pltpu.SemaphoreType.DMA((copies,)),
+            pltpu.SemaphoreType.DMA((copies,)),
+        ],
+        compiler_params=pltpu.CompilerParams(
+            collective_id=0, has_side_effects=True, vmem_limit_bytes=32 * 1024 * 1024
+        ),
+        name="sum_weights",
+    )(partial)
 
 
 def correlation(query_pos, support_pos, slot_masks, kernel_points):
@@ -42,19 +245,11 @@
     rounds = lax.axis_size("dom").bit_length() - 1
     send_table = send_leaf[0, 0]
     bound_count = send_table.shape[1]
-    send_feats = leaf_feats[send_table]
-    send_pos = positions[:, send_table].astype(jnp.bfloat16)
     got_feats = []
     got_pos = []
-    all_feats, all_pos = (
-        lax.all_gather(send_feats[None], "dom", axis=0, tiled=True),
-        lax.all_gather(send_pos[None], "dom", axis=0, tiled=True),
-    )
-    own_index = lax.axis_index("dom")
     for bit_index in range(rounds):
-        partner = jnp.bitwise_xor(own_index, 1 << bit_index)
-        got_feats.append(lax.dynamic_index_in_dim(all_feats, partner, 0, keepdims=False)[bit_index])
-        got_pos.append(lax.dynamic_index_in_dim(all_pos, partner, 0, keepdims=False)[:, bit_index])
+        got_feats.append(swapped(leaf_feats[send_table[bit_index]], "dom", bit_index))
+        got_pos.append(swapped(positions[:, send_table[bit_index]].astype(jnp.bfloat16), "dom", bit_index))
     pool_feats = jnp.concatenate([leaf_feats] + got_feats, 0)
     pool_pos = jnp.concatenate([positions] + [piece.astype(jnp.float32) for piece in got_pos], 1)
     slot_table = support_slot[0]
@@ -85,10 +280,11 @@
     ).astype(jnp.bfloat16)
     grad_local = jnp.einsum(
         "lkic,lio->kco", summed_low, upstream, preferred_element_type=jnp.float32
-    )
-    devices = lax.axis_size("dom") * lax.axis_size("rep")
-    grad_flat = grad_local.reshape(kernels * channels, -1)
-    grad_weight = lax.psum(grad_flat, ("dom", "rep")) / devices
+    ).astype(jnp.bfloat16)
+    halves = grad_local.reshape(kernels, channels, CORES, -1).transpose(2, 0, 1, 3)
+    nx, nz = lax.axis_size("rep") // CORES, lax.axis_size("dom") // NY
+    total = summed_weights(halves, nx, nz)
+    grad_weight = total.transpose(1, 2, 0, 3).reshape(kernels * channels, -1).astype(jnp.float32)
     grad_support = jnp.einsum(
         "lnkij,lkic->lnjc", correlated, grad_summed, preferred_element_type=jnp.float32
     )
@@ -106,14 +302,13 @@
     grad_leaves = grad_pool[:leaf_count]
     for bit_index in range(rounds):
         offset = leaf_count + bit_index * bound_count
-        returned = swapped(grad_pool[offset : offset + bound_count], "dom", bit_index)
+        returned = swapped(grad_pool[offset : offset + bound_count].astype(jnp.bfloat16), "dom", bit_index)
         back_select = (
             jnp.arange(leaf_count, dtype=jnp.int32)[:, None] == send_table[bit_index][None, :]
-        ).astype(jnp.float32)
+        ).astype(jnp.bfloat16)
         grad_leaves = grad_leaves + jnp.dot(
             back_select,
             returned.reshape(bound_count, -1),
-            precision=lax.Precision.HIGHEST,
             preferred_element_type=jnp.float32,
         ).reshape(leaf_count, points, channels)
     return (output[None], grad_leaves.astype(jnp.bfloat16)[None], grad_weight)

time: 413 us -> 145 us (0.35)
  waiting for transfers between devices: 300 us -> 0.04 us
  Pallas kernels: 0 us -> 44.7 us
  blocking collectives: 43.3 us -> 0 us
  local copies, waits for them, and re-layouts: 16.4 us -> 43.6 us
  starting transfers between devices: 6.95 us -> 27.7 us
  between operations: 14.5 us -> 1.01 us
    psum x1 -> x0, waiting for transfers between devices: 246 us -> none  [shards(): grad_weight = lax.psum(grad_flat, ('dom', 'rep')) / devices]
    all_gather x1 -> x0, waiting for transfers between devices: 48.5 us -> none  [shards(): lax.all_gather(send_feats[None], 'dom', axis=0, tiled=True)]
    pallas_call x0 -> x1, Pallas kernels: none -> 44.7 us  [summed_weights(): pl.pallas_call(functools.partial(sum_kernel, nx, nz, kernels), out_shape=...]
    all_gather x1 -> x0, blocking collectives: 43.3 us -> none  [shards(): lax.all_gather(send_pos[None], 'dom', axis=0, tiled=True)]
    ppermute x5 -> x15, starting transfers between devices: 6.87 us -> 27.7 us  [swapped(): return lax.ppermute(block, axis, route)]
    unnamed x29 -> x36, local copies, waits for them, and re-layouts: 6.16 us -> 15.9 us
    gather x2 -> x10, local copies, waits for them, and re-layouts: 2.81 us -> 11.1 us  [the longest x5 8.24 us: shards(): leaf_feats[send_table[bit_index]]]
    ppermute x5 -> x15, waiting for transfers between devices: 5.76 us -> 0.04 us  [swapped(): return lax.ppermute(block, axis, route)]
  transfers between devices with their start and end apart: 7 -> 15, of which waited for: 4 -> 0; matrix products, arithmetic and copies ran while one was open for 6% -> 45% of each run, Pallas kernels for 0% -> 31%
where the time goes in v1:
time: 145 us; the launch traced here: 144 us
  Pallas kernels  44.7 us (31%)
  local copies, waits for them, and re-layouts  43.6 us (30%)
  starting transfers between devices  27.7 us (19%)
  matrix products  15.8 us (11%)
  other arithmetic  11.6 us (8%)
    pallas_call x1, Pallas kernels, summed_weights(): pl.pallas_call(functools.partial(sum_kernel, nx, nz, kernels), out_shape=...  44.7 us
    ppermute x15, starting transfers between devices, swapped(): return lax.ppermute(block, axis, route)  27.7 us
    unnamed x36, local copies, waits for them, and re-layouts  15.9 us
    gather x5, local copies, waits for them, and re-layouts, shards(): leaf_feats[send_table[bit_index]]  8.24 us
    convert_element_type x1, other arithmetic, correlation(): return weight_map.astype(jnp.bfloat16)  7.14 us
    dot_general x5, matrix products, shards(): jnp.dot(back_select, returned.reshape(bound_count, -1), preferred_element...  4.17 us
    reshape x1, local copies, waits for them, and re-layouts, shards(): grad_local.reshape(kernels, channels, CORES, -1).transpose(2, 0, 1, 3)  3.96 us
    dot_general x1, matrix products, shards(): jnp.einsum('lnkij,lkic->lnjc', correlated, grad_summed, preferred_element...  3.96 us
  transfers between devices with their start and end apart: 15, of which 0 were waited for; matrix products, arithmetic and copies ran while one was open for 45% of the time, Pallas kernels for 31%

profile of v1, /device:TPU:1, one launch (start us, length us, event | category | flops | bytes accessed | tf_op | source)
XLA Modules:
  0.0 144.5 jit_solution(10757846528476611987)
XLA Ops:
  0.7 1.2 slice_reduce_fusion.3
  1.9 0.7 convert_multiply_fusion
  3.2 2.2 %collective-permute-start = (bf16[3,2,64]{2,0,1:T(4,128)(2,1)S(1)}, bf16[3,2,64]{2,0,1:T(4,128)(2,1)S(1)}, u32[]{:S(2)}, u32[]{:S(2)}) collective-permute-start(bf16[3,2,64]{2,0,1:T(4,128)(2,1)S(1)} %bitcast.253), channel_id=1, source_target_pairs={{0,8},{8,0},{16,24},{24,16},{32,40},{40,32},{48,56},{56,48},{64,72... | collective-permute-start | bytes 2312 | tf_op jit(solution)/shard_map/ppermute | solution.py:24
  6.0 7.0 %collective-permute-start.4 = (bf16[3,2,64]{2,0,1:T(4,128)(2,1)S(1)}, bf16[3,2,64]{2,0,1:T(4,128)(2,1)S(1)}, u32[]{:S(2)}, u32[]{:S(2)}) collective-permute-start(bf16[3,2,64]{2,0,1:T(4,128)(2,1)S(1)} %bitcast.252), channel_id=1, source_target_pairs={{0,128},{128,0},{8,136},{136,8},{16,144},{144,16},{24,152},{152,24... | collective-permute-start | bytes 2312 | tf_op jit(solution)/shard_map/ppermute | solution.py:24
  13.6 2.7 %collective-permute-start.1 = (bf16[3,2,64]{2,0,1:T(4,128)(2,1)S(1)}, bf16[3,2,64]{2,0,1:T(4,128)(2,1)S(1)}, u32[]{:S(2)}, u32[]{:S(2)}) collective-permute-start(bf16[3,2,64]{2,0,1:T(4,128)(2,1)S(1)} %bitcast.255), channel_id=1, source_target_pairs={{0,16},{16,0},{8,24},{24,8},{32,48},{48,32},{40,56},{56,40},{64,80... | collective-permute-start | bytes 2312 | tf_op jit(solution)/shard_map/ppermute | solution.py:24
  16.9 0.8 collective-permute-start.2
  18.3 1.3 collective-permute-start.3
  19.5 0.8 slice_bitcast_fusion.2
  20.3 0.7 compare_select_fusion
  21.1 1.0 fusion.18
  22.2 1.6 %constant_dynamic-update-slice_fusion.11 = bf16[14,64,256]{2,1,0:T(8,128)(2,1)} fusion(bf16[1,4,64,256]{3,2,1,0:T(8,128)(2,1)} %param.8), kind=kLoop, calls=%fused_computation.76 | loop fusion | bytes 262144
  23.7 1.1 fusion.12
  24.9 0.8 eq.91
  25.7 1.5 %gather_fusion.13 = bf16[2,64,256]{2,1,0:T(8,128)(2,1)S(1)} fusion(bf16[4,64,256]{2,1,0:T(8,128)(2,1)} %bitcast.220, s32[1024]{0:T(1024)S(1)} %pad_clamp_fusion.5), kind=kCustom, calls=%fused_computation.13 | custom fusion | bytes 131080 | tf_op jit(solution)/shard_map/gather | solution.py:251
  27.2 2.1 %gather_fusion.9 = bf16[2,64,256]{2,1,0:T(8,128)(2,1)} fusion(bf16[4,64,256]{2,1,0:T(8,128)(2,1)} %bitcast.221, s32[1024]{0:T(1024)S(1)} %pad_clamp_fusion.9), kind=kCustom, calls=%fused_computation.9 | custom fusion | bytes 131080 | tf_op jit(solution)/shard_map/gather | solution.py:251
  29.2 2.1 %gather_fusion.10 = bf16[2,64,256]{2,1,0:T(8,128)(2,1)} fusion(bf16[4,64,256]{2,1,0:T(8,128)(2,1)} %bitcast.222, s32[1024]{0:T(1024)S(1)} %pad_clamp_fusion.8), kind=kCustom, calls=%fused_computation.10 | custom fusion | bytes 131080 | tf_op jit(solution)/shard_map/gather | solution.py:251
  31.3 2.1 %gather_fusion.11 = bf16[2,64,256]{2,1,0:T(8,128)(2,1)} fusion(bf16[4,64,256]{2,1,0:T(8,128)(2,1)} %bitcast.223, s32[1024]{0:T(1024)S(1)} %pad_clamp_fusion.7), kind=kCustom, calls=%fused_computation.11 | custom fusion | bytes 131080 | tf_op jit(solution)/shard_map/gather | solution.py:251
  34.2 1.2 collective-permute-start.8
  35.4 0.7 collective-permute-start.7
  39.7 7.1 %multiply_convert_fusion.3 = (bf16[4,1,15,64,64]{4,3,1,2,0:T(8,128)(2,1)}, bf16[4,1,15,64,64]{4,3,1,2,0:T(8,128)(2,1)}, bf16[4,1,15,64,64]{4,3,1,2,0:T(8,128)(2,1)}, bf16[4,1,15,64,64]{4,3,1,2,0:T(8,128)(2,1)}) fusion(f32[4,64,64]{2,1,0:T(8,128)S(1)} %get-tuple-element.29, f32[15]{0:T(128)S(1)} %get-tuple-element.60, f32[4,64,64]{2,1,0:T(8,128)S(1)} %get-tuple-element.55, ...), kind=kLoop, calls=%fused_computation.27 | loop fusion | flops 12779520 | bytes 3014836 | tf_op jit(solution)/shard_map/convert_element_type | solution.py:237
  46.8 4.0 %fusion = f32[4,4,64,256,1]{3,2,1,4,0:T(8,128)S(1)} fusion(bf16[15,256,256,1]{2,1,0,3:T(8,128)(2,1)S(1)} %bitcast.214, bf16[4,1,15,64,64]{4,3,1,2,0:T(8,128)(2,1)} %get-tuple-element.65, bf16[4,1,15,64,64]{4,3,1,2,0:T(8,128)(2,1)} %get-tuple-element.64, bf16[4,1,15,64,64]{4,3,1,2,0:T(8,128)(2,1)} %get-tuple-element.63, ...), kind=kOutput, calls=%fused_computation.20 | convolution fusion | flops 1010565120 | bytes 5111808 | tf_op jit(solution)/shard_map/lnkij,lkic->lnjc/dot_general | solution.py:288
  52.3 0.6 copy.80
  52.9 0.6 copy.81
  53.5 0.6 copy.82
  54.8 0.6 copy.84
  55.5 1.2 collective-permute-start.10
  56.6 1.5 %constant_dynamic-update-slice_fusion.10 = bf16[14,64,256]{2,1,0:T(8,128)(2,1)} fusion(bf16[14,64,256]{2,1,0:T(8,128)(2,1)} %constant_dynamic-update-slice_fusion.11, bf16[2,64,256]{2,1,0:T(8,128)(2,1)} %collective-permute-done.5), kind=kLoop, calls=%fused_computation.75 | loop fusion | bytes 131072
  58.1 2.6 %collective-permute-start.11 = (bf16[2,64,256]{2,1,0:T(8,128)(2,1)}, bf16[2,64,256]{2,1,0:T(8,128)(2,1)}, u32[]{:S(2)}, u32[]{:S(2)}) collective-permute-start(bf16[2,64,256]{2,1,0:T(8,128)(2,1)} %bitcast.211), channel_id=1, source_target_pairs={{0,16},{16,0},{8,24},{24,8},{32,48},{48,32},{40,56},{56,40},{64,80... | collective-permute-start | bytes 196616 | tf_op jit(solution)/shard_map/ppermute | solution.py:24
  60.7 1.5 %constant_dynamic-update-slice_fusion.9 = bf16[14,64,256]{2,1,0:T(8,128)(2,1)} fusion(bf16[14,64,256]{2,1,0:T(8,128)(2,1)} %constant_dynamic-update-slice_fusion.10, bf16[2,64,256]{2,1,0:T(8,128)(2,1)} %collective-permute-done.6), kind=kLoop, calls=%fused_computation.74 | loop fusion | bytes 131072
  62.2 0.8 collective-permute-start.12
  63.0 1.5 %constant_dynamic-update-slice_fusion.8 = bf16[14,64,256]{2,1,0:T(8,128)(2,1)} fusion(bf16[14,64,256]{2,1,0:T(8,128)(2,1)} %constant_dynamic-update-slice_fusion.9, bf16[2,64,256]{2,1,0:T(8,128)(2,1)} %collective-permute-done.7), kind=kLoop, calls=%fused_computation.73 | loop fusion | bytes 131072
  64.5 2.3 %collective-permute-start.13 = (bf16[2,64,256]{2,1,0:T(8,128)(2,1)}, bf16[2,64,256]{2,1,0:T(8,128)(2,1)S(1)}, u32[]{:S(2)}, u32[]{:S(2)}) collective-permute-start(bf16[2,64,256]{2,1,0:T(8,128)(2,1)} %bitcast.209), channel_id=1, source_target_pairs={{0,64},{64,0},{8,72},{72,8},{16,80},{80,16},{24,88},{88,24},{32,96... | collective-permute-start | bytes 196616 | tf_op jit(solution)/shard_map/ppermute | solution.py:24
  67.4 4.2 %collective-permute-start.14 = (bf16[2,64,256]{2,1,0:T(8,128)(2,1)}, bf16[2,64,256]{2,1,0:T(8,128)(2,1)S(1)}, u32[]{:S(2)}, u32[]{:S(2)}) collective-permute-start(bf16[2,64,256]{2,1,0:T(8,128)(2,1)} %bitcast.208), channel_id=1, source_target_pairs={{0,128},{128,0},{8,136},{136,8},{16,144},{144,16},{24,152},{152,24... | collective-permute-start | bytes 196616 | tf_op jit(solution)/shard_map/ppermute | solution.py:24
  71.6 1.5 %constant_dynamic-update-slice_fusion.6 = bf16[14,64,256]{2,1,0:T(8,128)(2,1)} fusion(bf16[14,64,256]{2,1,0:T(8,128)(2,1)} %constant_dynamic-update-slice_fusion.7, bf16[2,64,256]{2,1,0:T(8,128)(2,1)} %collective-permute-done.9), kind=kLoop, calls=%fused_computation.71 | loop fusion | bytes 131072 | tf_op jit(solution)/shard_map/concatenate | solution.py:253
  73.0 2.4 %gather_fusion.14 = bf16[16,64,256]{2,1,0:T(8,128)(2,1)} fusion(bf16[14,64,256]{2,1,0:T(8,128)(2,1)} %constant_dynamic-update-slice_fusion.6, s32[1024]{0:T(1024)S(1)} %pad_clamp_fusion), kind=kCustom, calls=%fused_computation.14 | custom fusion | bytes 1048640 | tf_op jit(solution)/shard_map/gather | solution.py:257
  75.4 3.7 %bitcast_convert_fusion.1 = bf16[4,15,64,256]{3,2,1,0:T(8,128)(2,1)S(1)} fusion(bf16[4,4,64,256,1]{3,2,1,4,0:T(8,128)(2,1)} %bitcast.228, bf16[4,1,15,64,64]{4,3,1,2,0:T(8,128)(2,1)} %get-tuple-element.65, bf16[4,1,15,64,64]{4,3,1,2,0:T(8,128)(2,1)} %get-tuple-element.64, bf16[4,1,15,64,64]{4,3,1,2,0:T(8,128)(2,1)} %get-tuple-element.63, ...), kind=kOutput, calls=%fused_computation.18 | convolution fusion | flops 507248640 | bytes 4456448 | tf_op jit(solution)/shard_map/lnkij,lnjc->lkic/dot_general | solution.py:269
  79.1 2.0 %bitcast_convert_fusion = bf16[15,256,256]{1,2,0:T(8,128)(2,1)} fusion(bf16[4,15,64,256]{3,2,1,0:T(8,128)(2,1)S(1)} %bitcast_convert_fusion.1, bf16[1,4,64,256]{3,2,1,0:T(8,128)(2,1)S(1)} %copy-done.6), kind=kOutput, calls=%fused_computation.17 | convolution fusion | flops 504299520 | bytes 4063232 | tf_op jit(solution)/shard_map/lkic,lio->kco/dot_general | solution.py:281
  81.2 4.0 %copy.29 = bf16[15,256,2,128]{3,1,0,2:T(8,128)(2,1)} copy(bf16[15,256,2,128]{1,3,2,0:T(8,128)(2,1)} %bitcast.217) | data formatting | bytes 3932160 | tf_op jit(solution)/shard_map/reshape | solution.py:284
  85.2 1.5 %copy-done.1 = bf16[15,256,2,128]{3,1,0,2:T(8,128)(2,1)S(1)} copy-done((bf16[15,256,2,128]{3,1,0,2:T(8,128)(2,1)S(1)}, bf16[15,256,2,128]{3,1,0,2:T(8,128)(2,1)}, u32[]{:S(2)}) %copy-start.1) | copy-done | bytes 1966104
  86.7 44.7 %sum_weights.1 = bf16[2,15,256,128]{3,2,1,0:T(8,128)(2,1)S(1)} custom-call(bf16[2,15,256,128]{3,2,1,0:T(8,128)(2,1)S(1)} %bitcast.215), custom_call_target="tpu_custom_call" | custom-call | tf_op jit(solution)/shard_map/sum_weights/pallas_call | solution.py:197
  131.9 1.1 copy-done.3
  133.0 1.3 fusion.8
  134.3 3.0 %copy.30 = f32[15,256,2,128]{3,2,1,0:T(2,128)S(1)} copy(f32[15,256,2,128]{3,1,0,2:T(8,128)S(1)} %convert_bitcast_fusion) | data formatting | bytes 7864320 | tf_op jit(solution)/shard_map/convert_element_type | solution.py:287
  137.3 2.2 %copy.79 = f32[480,8,2,128]{3,1,2,0:T(8,128)} copy(f32[480,8,2,128]{3,2,1,0:T(2,128)S(1)} %bitcast.216) | data formatting | bytes 7864320
  139.5 1.2 convolution_add_fusion.4
  140.7 1.2 convolution_add_fusion.3
  141.9 1.2 convolution_add_fusion.2
  143.8 0.7 copy.31
  (88 shorter events, 11.3 us)
Async XLA Ops:
  0.6 46.2 %copy-start = (bf16[3840,256]{1,0:T(8,128)(2,1)S(1)}, bf16[3840,256]{1,0:T(8,128)(2,1)}, u32[]{:S(2)}) copy-start(bf16[3840,256]{1,0:T(8,128)(2,1)} %param.11) | copy-start | bytes 5898244
  0.6 32.7 %copy-start.4 = (bf16[1,4,64,256]{3,2,1,0:T(8,128)(2,1)S(1)}, bf16[1,4,64,256]{3,2,1,0:T(8,128)(2,1)}, u32[]{:S(2)}) copy-start(bf16[1,4,64,256]{3,2,1,0:T(8,128)(2,1)} %param.8) | copy-start | bytes 393220
  1.8 0.8 copy-start.7
  1.8 32.4 %copy-start.9 = (s32[2]{0:T(128)}, s32[2]{0:T(128)S(1)}, u32[]{:S(2)}) copy-start(s32[2]{0:T(128)S(1)} %get-tuple-element.19) | copy-start | bytes 28
  3.2 31.0 %collective-permute-start = (bf16[3,2,64]{2,0,1:T(4,128)(2,1)S(1)}, bf16[3,2,64]{2,0,1:T(4,128)(2,1)S(1)}, u32[]{:S(2)}, u32[]{:S(2)}) collective-permute-start(bf16[3,2,64]{2,0,1:T(4,128)(2,1)S(1)} %bitcast.253), channel_id=1, source_target_pairs={{0,8},{8,0},{16,24},{24,16},{32,40},{40,32},{48,56},{56,48},{64,72... | collective-permute-start | bytes 2312 | tf_op jit(solution)/shard_map/ppermute | solution.py:24
  6.0 30.7 %collective-permute-start.4 = (bf16[3,2,64]{2,0,1:T(4,128)(2,1)S(1)}, bf16[3,2,64]{2,0,1:T(4,128)(2,1)S(1)}, u32[]{:S(2)}, u32[]{:S(2)}) collective-permute-start(bf16[3,2,64]{2,0,1:T(4,128)(2,1)S(1)} %bitcast.252), channel_id=1, source_target_pairs={{0,128},{128,0},{8,136},{136,8},{16,144},{144,16},{24,152},{152,24... | collective-permute-start | bytes 2312 | tf_op jit(solution)/shard_map/ppermute | solution.py:24
  13.6 21.8 %collective-permute-start.1 = (bf16[3,2,64]{2,0,1:T(4,128)(2,1)S(1)}, bf16[3,2,64]{2,0,1:T(4,128)(2,1)S(1)}, u32[]{:S(2)}, u32[]{:S(2)}) collective-permute-start(bf16[3,2,64]{2,0,1:T(4,128)(2,1)S(1)} %bitcast.255), channel_id=1, source_target_pairs={{0,16},{16,0},{8,24},{24,8},{32,48},{48,32},{40,56},{56,40},{64,80... | collective-permute-start | bytes 2312 | tf_op jit(solution)/shard_map/ppermute | solution.py:24
  16.9 19.3 %collective-permute-start.2 = (bf16[3,2,64]{2,0,1:T(4,128)(2,1)S(1)}, bf16[3,2,64]{2,0,1:T(4,128)(2,1)S(1)}, u32[]{:S(2)}, u32[]{:S(2)}) collective-permute-start(bf16[3,2,64]{2,0,1:T(4,128)(2,1)S(1)} %bitcast.256), channel_id=1, source_target_pairs={{0,32},{32,0},{8,40},{40,8},{16,48},{48,16},{24,56},{56,24},{64,96... | collective-permute-start | bytes 2312 | tf_op jit(solution)/shard_map/ppermute | solution.py:24
  18.3 18.3 %collective-permute-start.3 = (bf16[3,2,64]{2,0,1:T(4,128)(2,1)S(1)}, bf16[3,2,64]{2,0,1:T(4,128)(2,1)S(1)}, u32[]{:S(2)}, u32[]{:S(2)}) collective-permute-start(bf16[3,2,64]{2,0,1:T(4,128)(2,1)S(1)} %bitcast.254), channel_id=1, source_target_pairs={{0,64},{64,0},{8,72},{72,8},{16,80},{80,16},{24,88},{88,24},{32,96... | collective-permute-start | bytes 2312 | tf_op jit(solution)/shard_map/ppermute | solution.py:24
  34.2 30.3 %collective-permute-start.8 = (bf16[2,64,256]{2,1,0:T(8,128)(2,1)S(1)}, bf16[2,64,256]{2,1,0:T(8,128)(2,1)S(1)}, u32[]{:S(2)}, u32[]{:S(2)}) collective-permute-start(bf16[2,64,256]{2,1,0:T(8,128)(2,1)S(1)} %gather_fusion.12), channel_id=1, source_target_pairs={{0,64},{64,0},{8,72},{72,8},{16,80},{80,16},{24,88},{88,24},{32,96... | collective-permute-start | bytes 196616 | tf_op jit(solution)/shard_map/ppermute | solution.py:24
  35.4 26.8 %collective-permute-start.7 = (bf16[2,64,256]{2,1,0:T(8,128)(2,1)}, bf16[2,64,256]{2,1,0:T(8,128)(2,1)}, u32[]{:S(2)}, u32[]{:S(2)}) collective-permute-start(bf16[2,64,256]{2,1,0:T(8,128)(2,1)} %gather_fusion.11), channel_id=1, source_target_pairs={{0,32},{32,0},{8,40},{40,8},{16,48},{48,16},{24,56},{56,24},{64,96... | collective-permute-start | bytes 196616 | tf_op jit(solution)/shard_map/ppermute | solution.py:24
  36.2 21.9 %collective-permute-start.6 = (bf16[2,64,256]{2,1,0:T(8,128)(2,1)}, bf16[2,64,256]{2,1,0:T(8,128)(2,1)}, u32[]{:S(2)}, u32[]{:S(2)}) collective-permute-start(bf16[2,64,256]{2,1,0:T(8,128)(2,1)} %gather_fusion.10), channel_id=1, source_target_pairs={{0,16},{16,0},{8,24},{24,8},{32,48},{48,32},{40,56},{56,40},{64,80... | collective-permute-start | bytes 196616 | tf_op jit(solution)/shard_map/ppermute | solution.py:24
  36.5 18.9 %collective-permute-start.5 = (bf16[2,64,256]{2,1,0:T(8,128)(2,1)}, bf16[2,64,256]{2,1,0:T(8,128)(2,1)}, u32[]{:S(2)}, u32[]{:S(2)}) collective-permute-start(bf16[2,64,256]{2,1,0:T(8,128)(2,1)} %gather_fusion.9), channel_id=1, source_target_pairs={{0,8},{8,0},{16,24},{24,16},{32,40},{40,32},{48,56},{56,48},{64,72... | collective-permute-start | bytes 196616 | tf_op jit(solution)/shard_map/ppermute | solution.py:24
  36.7 30.6 %collective-permute-start.9 = (bf16[2,64,256]{2,1,0:T(8,128)(2,1)S(1)}, bf16[2,64,256]{2,1,0:T(8,128)(2,1)}, u32[]{:S(2)}, u32[]{:S(2)}) collective-permute-start(bf16[2,64,256]{2,1,0:T(8,128)(2,1)S(1)} %gather_fusion.13), channel_id=1, source_target_pairs={{0,128},{128,0},{8,136},{136,8},{16,144},{144,16},{24,152},{152,24... | collective-permute-start | bytes 196616 | tf_op jit(solution)/shard_map/ppermute | solution.py:24
  39.7 7.2 %copy-start.6 = (bf16[1,4,64,256]{3,2,1,0:T(8,128)(2,1)S(1)}, bf16[1,4,64,256]{3,2,1,0:T(8,128)(2,1)}, u32[]{:S(2)}) copy-start(bf16[1,4,64,256]{3,2,1,0:T(8,128)(2,1)} %param.15) | copy-start | bytes 393220
  52.0 23.4 %copy-start.5 = (bf16[4,1,15,64,64]{4,3,1,2,0:T(8,128)(2,1)S(1)}, bf16[4,1,15,64,64]{4,3,1,2,0:T(8,128)(2,1)}, u32[]{:S(2)}) copy-start(bf16[4,1,15,64,64]{4,3,1,2,0:T(8,128)(2,1)} %get-tuple-element.62) | copy-start | bytes 1474564
  55.5 84.1 %collective-permute-start.10 = (bf16[2,64,256]{2,1,0:T(8,128)(2,1)}, bf16[2,64,256]{2,1,0:T(8,128)(2,1)}, u32[]{:S(2)}, u32[]{:S(2)}) collective-permute-start(bf16[2,64,256]{2,1,0:T(8,128)(2,1)} %bitcast.212), channel_id=1, source_target_pairs={{0,8},{8,0},{16,24},{24,16},{32,40},{40,32},{48,56},{56,48},{64,72... | collective-permute-start | bytes 196616 | tf_op jit(solution)/shard_map/ppermute | solution.py:24
  58.1 82.6 %collective-permute-start.11 = (bf16[2,64,256]{2,1,0:T(8,128)(2,1)}, bf16[2,64,256]{2,1,0:T(8,128)(2,1)}, u32[]{:S(2)}, u32[]{:S(2)}) collective-permute-start(bf16[2,64,256]{2,1,0:T(8,128)(2,1)} %bitcast.211), channel_id=1, source_target_pairs={{0,16},{16,0},{8,24},{24,8},{32,48},{48,32},{40,56},{56,40},{64,80... | collective-permute-start | bytes 196616 | tf_op jit(solution)/shard_map/ppermute | solution.py:24
  62.2 79.7 %collective-permute-start.12 = (bf16[2,64,256]{2,1,0:T(8,128)(2,1)}, bf16[2,64,256]{2,1,0:T(8,128)(2,1)}, u32[]{:S(2)}, u32[]{:S(2)}) collective-permute-start(bf16[2,64,256]{2,1,0:T(8,128)(2,1)} %bitcast.210), channel_id=1, source_target_pairs={{0,32},{32,0},{8,40},{40,8},{16,48},{48,16},{24,56},{56,24},{64,96... | collective-permute-start | bytes 196616 | tf_op jit(solution)/shard_map/ppermute | solution.py:24
  64.5 78.6 %collective-permute-start.13 = (bf16[2,64,256]{2,1,0:T(8,128)(2,1)}, bf16[2,64,256]{2,1,0:T(8,128)(2,1)S(1)}, u32[]{:S(2)}, u32[]{:S(2)}) collective-permute-start(bf16[2,64,256]{2,1,0:T(8,128)(2,1)} %bitcast.209), channel_id=1, source_target_pairs={{0,64},{64,0},{8,72},{72,8},{16,80},{80,16},{24,88},{88,24},{32,96... | collective-permute-start | bytes 196616 | tf_op jit(solution)/shard_map/ppermute | solution.py:24
  67.4 76.1 %collective-permute-start.14 = (bf16[2,64,256]{2,1,0:T(8,128)(2,1)}, bf16[2,64,256]{2,1,0:T(8,128)(2,1)S(1)}, u32[]{:S(2)}, u32[]{:S(2)}) collective-permute-start(bf16[2,64,256]{2,1,0:T(8,128)(2,1)} %bitcast.208), channel_id=1, source_target_pairs={{0,128},{128,0},{8,136},{136,8},{16,144},{144,16},{24,152},{152,24... | collective-permute-start | bytes 196616 | tf_op jit(solution)/shard_map/ppermute | solution.py:24
  79.1 2.1 %copy-start.2 = (bf16[4,15,64,256]{3,2,1,0:T(8,128)(2,1)}, bf16[4,15,64,256]{3,2,1,0:T(8,128)(2,1)S(1)}, u32[]{:S(2)}) copy-start(bf16[4,15,64,256]{3,2,1,0:T(8,128)(2,1)S(1)} %bitcast_convert_fusion.1) | copy-start | bytes 5898244
  85.2 1.5 %copy-start.1 = (bf16[15,256,2,128]{3,1,0,2:T(8,128)(2,1)S(1)}, bf16[15,256,2,128]{3,1,0,2:T(8,128)(2,1)}, u32[]{:S(2)}) copy-start(bf16[15,256,2,128]{3,1,0,2:T(8,128)(2,1)} %copy.29) | copy-start | bytes 5898244
  131.4 1.5 %copy-start.3 = (bf16[4,15,64,256]{3,2,1,0:T(8,128)(2,1)S(1)}, bf16[4,15,64,256]{3,2,1,0:T(8,128)(2,1)}, u32[]{:S(2)}) copy-start(bf16[4,15,64,256]{3,2,1,0:T(8,128)(2,1)} %copy-done.2) | copy-start | bytes 5898244
  137.3 2.2 %copy-start.8 = (s32[2]{0:T(128)S(1)}, s32[2]{0:T(128)}, u32[]{:S(2)}) copy-start(s32[2]{0:T(128)} %copy-done.7) | copy-start | bytes 28
  139.5 3.9 %copy-start.10 = (s32[2]{0:T(128)S(1)}, s32[2]{0:T(128)}, u32[]{:S(2)}) copy-start(s32[2]{0:T(128)} %copy-done.9) | copy-start | bytes 28

commit v2 on v0

v2 whole, which is shorter than its diff:
```python
import functools

import jax
import jax.numpy as jnp
from jax import lax
from jax.experimental import pallas as pl
from jax.experimental.pallas import tpu as pltpu
from jax.sharding import PartitionSpec as P

QUANT = 0.0625
EPSILON = 1e-06
CORES = 2
NY = 4
CHUNK = 8
MESH = pl.DeviceIdType.MESH
F32, BF16 = jnp.float32, jnp.bfloat16


def place():
    dom, rep = lax.axis_index("dom"), lax.axis_index("rep")
    return rep // CORES, lax.rem(dom, NY), dom // NY, lax.rem(rep, CORES)


def device(x, y, z, core):
    return (z * NY + y, x * CORES + core)


def greet(others):
    barrier = pltpu.get_barrier_semaphore()
    for other in others:
        pl.semaphore_signal(barrier, inc=1, device_id=other, device_id_type=MESH)
    return lambda: pl.semaphore_wait(barrier, len(others))


def around(position, count):
    return [lax.rem(position + step, count) for step in range(1, count)]


def product(left, right, dims):
    return lax.dot_general(left, right, (dims, ((), ())), preferred_element_type=F32)


def copy_counts(nx, nz, kernels, rounds):
    chunks = -(-kernels // CHUNK)
    return 3 * rounds + 1 + chunks * (2 + 4 * (nx - 1) + 4 * (NY - 1) + 2 * (nz - 1))


def kernel(
    nx, nz, kernels, rounds,
    feats, coords, kernel_points, weights_hbm, slots, mask_hbm, sends, cot,
    output, grad, final,
    weights, mask, pool_feats, pool_pos, own_pos, send_feats, send_pos, query, cot_pair, h, grad_summed, grad_support,
    send_grad, got_grad, support, summed, summed_pair, out_sum, partial, got_first, part, got_second,
    slab, got_z, piece, gather_z, gather_second,
    local_sem, send_sem, recv_sem,
):
    leaves, points, channels = feats.shape
    near = slots.shape[1]
    bound = sends.shape[1]
    x, y, z, core = place()
    dom = z * NY + y
    sibling = device(x, y, z, 1 - core)
    axes = {
        "x": (x, nx, lambda o: device(o, y, z, core)),
        "y": (y, NY, lambda o: device(x, o, z, core)),
        "z": (z, nz, lambda o: device(x, y, o, core)),
    }
    low = NY.bit_length() - 1
    partners = []
    for bit in range(rounds):
        if bit < low:
            side = 1 << bit
            partners.append(device(x, y + side - 2 * side * lax.rem(y // side, 2), z, core))
        else:
            side = 1 << (bit - low)
            partners.append(device(x, y, z + side - 2 * side * lax.rem(z // side, 2), core))
    others = [sibling]
    for at, count, to in axes.values():
        others += [to(o) for o in around(at, count)]
    all_here = greet(others)

    load_weights = pltpu.make_async_copy(weights_hbm, weights, local_sem.at[0])
    load_weights.start()
    load_mask = pltpu.make_async_copy(mask_hbm, mask, local_sem.at[1])
    load_mask.start()

    number = [0]
    started = []

    def push(src, dst, other):
        index = number[0]
        number[0] += 1
        copy = pltpu.make_async_remote_copy(
            src_ref=src, dst_ref=dst, send_sem=send_sem.at[index], recv_sem=recv_sem.at[index],
            device_id=other, device_id_type=MESH,
        )
        copy.start()
        started.append(copy)
        return copy

    def arrive(copies):
        for copy in copies:
            copy.wait_recv()

    positions = coords[...].astype(F32) * QUANT
    for leaf in range(leaves):
        own = positions[:, leaf * points : (leaf + 1) * points]
        both = jnp.concatenate([own, own], 1)
        own_pos[leaf] = jnp.concatenate([both, jnp.zeros((8 - 3, 2 * points), F32)], 0)
        pool_pos[leaf] = own_pos[leaf]
        pool_feats[leaf] = feats[leaf]
    for bit in range(rounds):
        for t in range(bound):
            chosen = sends[bit, t]
            send_feats[bit * bound + t] = feats[chosen]
            send_pos[bit * bound + t] = own_pos[chosen]
    all_here()
    copies_pos, copies_feats = [], []
    for bit in reversed(range(rounds)):
        entry, there = pl.ds(bit * bound, bound), pl.ds(leaves + bit * bound, bound)
        copies_pos.append(push(send_pos.at[entry], pool_pos.at[there], partners[bit]))
    for bit in reversed(range(rounds)):
        entry, there = pl.ds(bit * bound, bound), pl.ds(leaves + bit * bound, bound)
        copies_feats.append(push(send_feats.at[entry], pool_feats.at[there], partners[bit]))
    copy_cot = push(cot, cot_pair, sibling)

    rows = lax.broadcasted_iota(jnp.int32, (points, 2 * points), 0)
    lanes = lax.broadcasted_iota(jnp.int32, (points, 2 * points), 1)
    for leaf in range(leaves):
        for c in range(3):
            line = jnp.where(rows == lanes, pool_pos[leaf, c : c + 1, :], 0.0)
            query[c, leaf] = jnp.broadcast_to(jnp.sum(line, 1, keepdims=True), (points, 2 * points))

    load_weights.wait()

    def grads(k, _):
        block = product(cot[...].reshape(leaves * points, channels), weights[k], ((1,), (1,)))
        grad_summed[:, k] = block.astype(BF16).reshape(leaves, points, channels)
        return 0

    lax.fori_loop(0, kernels, grads, 0)

    load_mask.wait()
    arrive(copies_pos)
    unroll = 3 if kernels % 3 == 0 else 1

    def correlate(leaf, _):
        for pair in range(near // 2):
            first = pool_pos[slots[leaf, 2 * pair]]
            second = pool_pos[slots[leaf, 2 * pair + 1]]
            lane = lax.broadcasted_iota(jnp.int32, first.shape, 1)
            places = jnp.where(lane < points, first, second)
            apart = [places[c : c + 1, :] - query[c, leaf] for c in range(3)]
            shown = jnp.concatenate([mask[leaf, 2 * pair], mask[leaf, 2 * pair + 1]], 1).astype(F32)

            def one(step, _):
                for k in [step * unroll + u for u in range(unroll)]:
                    squared = jnp.full(shown.shape, EPSILON, F32)
                    for c in range(3):
                        difference = apart[c] - kernel_points[k, c]
                        squared = squared + difference * difference
                    weight = jnp.maximum(1.0 - squared * lax.rsqrt(squared), 0.0) * shown
                    h[leaf, k, :, pair * 2 * points : (pair + 1) * 2 * points] = weight.astype(BF16)
                return 0

            lax.fori_loop(0, kernels // unroll, one, 0)
        return 0

    lax.fori_loop(0, leaves, correlate, 0)

    def supports(leaf, _):
        left = h[leaf].reshape(kernels * points, near * points)
        right = grad_summed[leaf].reshape(kernels * points, channels)
        grad_support[leaf] = product(left, right, ((0,), (0,)))
        return 0

    lax.fori_loop(0, leaves, supports, 0)

    def gathered(entry, total):
        for leaf in range(leaves):
            for n in range(1, near):
                named = jnp.where(slots[leaf, n] == entry, 1.0, 0.0)
                total = total + named * grad_support[leaf, n * points : (n + 1) * points, :]
        return total

    def away(entry, _):
        send_grad[entry] = gathered(entry + leaves, jnp.zeros((points, channels), F32)).astype(BF16)
        return 0

    lax.fori_loop(0, rounds * bound, away, 0)
    copies_grad = []
    for bit in reversed(range(rounds)):
        entry = pl.ds(bit * bound, bound)
        copies_grad.append(push(send_grad.at[entry], got_grad.at[entry], partners[bit]))

    half = channels // CORES
    own_half = pl.ds(pl.multiple_of(core * half, half), half)
    pair_half = pl.ds(pl.multiple_of((1 - core) * half, half), half)
    chunks = [(k0, min(CHUNK, kernels - k0)) for k0 in range(0, kernels, CHUNK)]
    arrive(copies_feats)
    for leaf in range(leaves):
        for n in range(near):
            support[leaf, n * points : (n + 1) * points, :] = pool_feats[slots[leaf, n]]
    copies_summed = []
    for k0, nk in chunks:

        def sums(leaf, _, k0=k0, nk=nk):
            left = h[leaf, k0 : k0 + nk].reshape(nk * points, near * points)
            block = product(left, support[leaf], ((1,), (0,))).astype(BF16)
            at = pl.ds(pl.multiple_of(leaf * points, points), points)
            summed[k0 : k0 + nk, at, :] = block.reshape(nk, points, channels)
            return 0

        lax.fori_loop(0, leaves, sums, 0)
        there = pl.ds(k0, nk)
        copies_summed.append(push(summed.at[there, :, pair_half], summed_pair.at[there], sibling))

    arrive([copy_cot])
    groups = []
    for k0, nk in chunks:
        cut = min(CHUNK // 2, nk)
        groups.append([(k0, cut, "x", "y"), (k0 + cut, nk - cut, "y", "x")])

    def band(axis, at):
        block = half // axes[axis][1]
        return pl.ds(pl.multiple_of(at * block, block), block)

    def tile(axis, at):
        block = part.shape[1] // (axes[axis][1] // 2)
        width = channels // 2
        down, across = at // 2, lax.rem(at, 2)
        return pl.ds(pl.multiple_of(down * block, block), block), pl.ds(pl.multiple_of(across * width, width), width)

    firsts = []
    for (k0, nk), copy, pieces in zip(chunks, copies_summed, groups):
        arrive([copy])

        def terms(k, _):
            block = product(summed[k, :, own_half], cot[...].reshape(leaves * points, channels), ((0,), (0,)))
            block += product(summed_pair[k], cot_pair[...].reshape(leaves * points, channels), ((0,), (0,)))
            partial[k] = block.astype(BF16)
            return 0

        sent = []
        for g0, ng, first, _ in pieces:
            lax.fori_loop(g0, g0 + ng, terms, 0)
            at, count, to = axes[first]
            there = pl.ds(g0, ng)
            sent.append([
                push(partial.at[there, band(first, o), :], got_first.at[step, there], to(o))
                for step, o in enumerate(around(at, count))
            ])
        firsts.append(sent)

    out_sum[...] = jnp.zeros(out_sum.shape, F32)

    def outputs(k, _):
        out_sum[...] += product(summed[k], weights[k], ((1,), (0,)))
        return 0

    lax.fori_loop(0, kernels, outputs, 0)
    output[...] = out_sum[...].astype(BF16).reshape(output.shape)

    seconds = []
    for sent, pieces in zip(firsts, groups):
        again = []
        for copies, (g0, ng, first, second) in zip(sent, pieces):
            arrive(copies)
            at, count, _ = axes[first]
            own = band(first, at)

            def add_first(k, _, own=own, count=count):
                total = partial[k, own, :].astype(F32)
                for step in range(count - 1):
                    total = total + got_first[step, k].astype(F32)
                part[k] = total.astype(BF16)
                return 0

            lax.fori_loop(g0, g0 + ng, add_first, 0)
            at, count, to = axes[second]
            there = pl.ds(g0, ng)
            again.append([
                push(part.at[there, *tile(second, o)], got_second.at[step, there], to(o))
                for step, o in enumerate(around(at, count))
            ])
        seconds.append(again)

    arrive(copies_grad)

    def owned(leaf, _):
        total = gathered(leaf, grad_support[leaf, 0:points, :])
        for bit in range(rounds):
            for t in range(bound):
                named = jnp.where(sends[bit, t] == leaf, 1.0, 0.0)
                total = total + named * got_grad[bit * bound + t].astype(F32)
        grad[leaf] = total.astype(BF16)
        return 0

    lax.fori_loop(0, leaves, owned, 0)

    per_z = CHUNK // nz
    for k in range(kernels, slab.shape[0]):
        slab[k] = jnp.zeros(slab.shape[1:], BF16)
    thirds = []
    for index, (again, pieces) in enumerate(zip(seconds, groups)):
        for copies, (g0, ng, _, second) in zip(again, pieces):
            arrive(copies)
            at, count, _ = axes[second]
            own = tile(second, at)

            def add_second(k, _, own=own, count=count):
                total = part[k, own[0], own[1]].astype(F32)
                for step in range(count - 1):
                    total = total + got_second[step, k].astype(F32)
                slab[k] = total.astype(BF16)
                return 0

            lax.fori_loop(g0, g0 + ng, add_second, 0)
        at, count, to = axes["z"]
        thirds.append([
            push(slab.at[pl.ds(index * CHUNK + o * per_z, per_z)], got_z.at[index, step], to(o))
            for step, o in enumerate(around(at, count))
        ])
    back_z = []
    for index, copies in enumerate(thirds):
        arrive(copies)
        at, count, to = axes["z"]
        own = pl.ds(index * CHUNK + z * per_z, per_z)
        total = slab[own].astype(F32)
        for step in range(count - 1):
            total = total + got_z[index, step].astype(F32)
        piece[index] = (total / (nx * NY * nz * CORES)).astype(BF16)
        back_z.append([push(piece.at[index], gather_z.at[own], to(o)) for o in around(at, count)])
        gather_z[own] = piece[index]
    back_second = []
    for copies, pieces in zip(back_z, groups):
        arrive(copies)
        sent = []
        for g0, ng, _, second in pieces:
            at, count, to = axes[second]
            there = pl.ds(g0, ng)
            own = tile(second, at)
            sent.append([
                push(gather_z.at[there], gather_second.at[there, *own], to(o)) for o in around(at, count)
            ])
            gather_second[there, own[0], own[1]] = gather_z[there]
        back_second.append(sent)
    back_first = []
    for sent, pieces in zip(back_second, groups):
        again = []
        for copies, (g0, ng, first, _) in zip(sent, pieces):
            arrive(copies)
            at, count, to = axes[first]
            there = pl.ds(g0, ng)
            block = half // count
            own = pl.ds(pl.multiple_of(core * half + at * block, block), block)
            again.append([
                push(gather_second.at[there], final.at[there, own, :], to(o)) for o in around(at, count)
            ])
            final[there, own, :] = gather_second[there]
        back_first.append(again)
    lasts = []
    for again, (k0, nk) in zip(back_first, chunks):
        for copies in again:
            arrive(copies)
        mine = final.at[pl.ds(k0, nk), own_half, :]
        lasts.append(push(mine, mine, sibling))
    arrive(lasts)
    for copy in started:
        copy.wait_send()


def shards(features, coords, kernel_points, weights, support_slot, slot_mask, send_leaf, cotangent):
    leaves, points, channels = features.shape[1:]
    kernels = kernel_points.shape[0]
    near = support_slot.shape[2]
    nx, nz = lax.axis_size("rep") // CORES, lax.axis_size("dom") // NY
    rounds = lax.axis_size("dom").bit_length() - 1
    bound = send_leaf.shape[3]
    received = rounds * bound
    chunks = -(-kernels // CHUNK)
    padded = chunks * CHUNK
    half = channels // CORES
    wide = max(nx, NY)
    band = half // min(nx, NY)
    tile = band // (wide // 2)
    width = channels // 2
    copies = copy_counts(nx, nz, kernels, rounds)
    vmem, smem, anywhere = (
        pl.BlockSpec(memory_space=space) for space in (pltpu.VMEM, pltpu.SMEM, pl.ANY)
    )
    cube = (kernels, channels, channels)
    leaf_shape = (leaves, points, channels)
    output, grad, mean = pl.pallas_call(
        functools.partial(kernel, nx, nz, kernels, rounds),
        out_shape=(
            jax.ShapeDtypeStruct(leaf_shape, BF16),
            jax.ShapeDtypeStruct(leaf_shape, BF16),
            jax.ShapeDtypeStruct(cube, BF16),
        ),
        in_specs=[vmem, vmem, smem, anywhere, smem, anywhere, smem, vmem],
        out_specs=(vmem, vmem, vmem),
        scratch_shapes=[
            pltpu.VMEM(cube, BF16),
            pltpu.VMEM(slot_mask.shape[1:], jnp.int32),
            pltpu.VMEM((leaves + received, points, channels), BF16),
            pltpu.VMEM((leaves + received, 8, 2 * points), F32),
            pltpu.VMEM((leaves, 8, 2 * points), F32),
            pltpu.VMEM((received, points, channels), BF16),
            pltpu.VMEM((received, 8, 2 * points), F32),
            pltpu.VMEM((3, leaves, points, 2 * points), F32),
            pltpu.VMEM(leaf_shape, BF16),
            pltpu.VMEM((leaves, kernels, points, near * points), BF16),
            pltpu.VMEM((leaves, kernels, points, channels), BF16),
            pltpu.VMEM((leaves, near * points, channels), F32),
            pltpu.VMEM((received, points, channels), BF16),
            pltpu.VMEM((received, points, channels), BF16),
            pltpu.VMEM((leaves, near * points, channels), BF16),
            pltpu.VMEM((kernels, leaves * points, channels), BF16),
            pltpu.VMEM((kernels, leaves * points, half), BF16),
            pltpu.VMEM((leaves * points, channels), F32),
            pltpu.VMEM((kernels, half, channels), BF16),
            pltpu.VMEM((wide - 1, kernels, band, channels), BF16),
            pltpu.VMEM((kernels, band, channels), BF16),
            pltpu.VMEM((wide - 1, kernels, tile, width), BF16),
            pltpu.VMEM((padded, tile, width), BF16),
            pltpu.VMEM((chunks, nz - 1, CHUNK // nz, tile, width), BF16),
            pltpu.VMEM((chunks, CHUNK // nz, tile, width), BF16),
            pltpu.VMEM((padded, tile, width), BF16),
            pltpu.VMEM((kernels, band, channels), BF16),
            pltpu.SemaphoreType.DMA((2,)),
            pltpu.SemaphoreType.DMA((copies,)),
            pltpu.SemaphoreType.DMA((copies,)),
        ],
        compiler_params=pltpu.CompilerParams(
            collective_id=0, has_side_effects=True, vmem_limit_bytes=48 * 1024 * 1024
        ),
        name="convolution",
    )(
        features[0], coords[0], kernel_points, weights.reshape(cube), support_slot[0], slot_mask[0],
        send_leaf[0, 0], cotangent[0],
    )
    grad_weight = mean.astype(F32).reshape(kernels * channels, channels)
    return (output[None], grad[None], grad_weight)


def solution(mesh):
    in_specs = (
        P("rep", "dom", None, None),
        P("rep", None, "dom"),
        P(),
        P(),
        P("rep", "dom", None),
        P("rep", "dom", None, None, None),
        P("rep", "dom", None, None),
        P("rep", "dom", None, None),
    )
    out_specs = (P("rep", "dom", None, None), P("rep", "dom", None, None), P())
    return jax.shard_map(shards, mesh=mesh, in_specs=in_specs, out_specs=out_specs, check_vma=False)
```

time: 413 us -> 72.2 us (0.17)
  waiting for transfers between devices: 300 us -> 0 us
  Pallas kernels: 0 us -> 60.3 us
  blocking collectives: 43.3 us -> 0 us
  matrix products: 15.2 us -> 0 us
  between operations: 14.5 us -> 0.65 us
  other arithmetic: 15.2 us -> 2.36 us
  local copies, waits for them, and re-layouts: 16.4 us -> 8.6 us
  starting transfers between devices: 6.95 us -> 0 us
    psum x1 -> x0, waiting for transfers between devices: 246 us -> none  [shards(): grad_weight = lax.psum(grad_flat, ('dom', 'rep')) / devices]
    pallas_call x0 -> x1, Pallas kernels: none -> 60.3 us  [shards(): pl.pallas_call(functools.partial(kernel, nx, nz, kernels, rounds), out_sh...]
    all_gather x1 -> x0, waiting for transfers between devices: 48.5 us -> none  [shards(): lax.all_gather(send_feats[None], 'dom', axis=0, tiled=True)]
    all_gather x1 -> x0, blocking collectives: 43.3 us -> none  [shards(): lax.all_gather(send_pos[None], 'dom', axis=0, tiled=True)]
    dot_general x10 -> x0, matrix products: 15.2 us -> none  [the longest x1 4 us: shards(): jnp.einsum('lnkij,lnjc->lkic', correlated, support_feats, preferred_eleme...]
    convert_element_type x1 -> x0, other arithmetic: 7.17 us -> none  [correlation(): return weight_map.astype(jnp.bfloat16)]
    ppermute x5 -> x0, starting transfers between devices: 6.87 us -> none  [swapped(): return lax.ppermute(block, axis, route)]
    gather x7 -> x0, local copies, waits for them, and re-layouts: 6.46 us -> none  [the longest x4 2.28 us: shards(): pool_pos[:, slot_table[:, slot_index]]]
  transfers between devices with their start and end apart: 7 -> 0, of which waited for: 4 -> 0; matrix products, arithmetic and copies ran while one was open for 6% -> 0% of each run, Pallas kernels for 0% -> 0%
where the time goes in v2:
time: 72.2 us; the launch traced here: 71.9 us
  Pallas kernels  60.3 us (84%)
  local copies, waits for them, and re-layouts  8.6 us (12%)
  other arithmetic  2.36 us (3%)
    pallas_call x1, Pallas kernels, shards(): pl.pallas_call(functools.partial(kernel, nx, nz, kernels, rounds), out_sh...  60.3 us
    unnamed x14, local copies, waits for them, and re-layouts  7.84 us
    reshape x1, other arithmetic, shards(): grad_weight = mean.astype(F32).reshape(kernels * channels, channels)  2.36 us

profile of v2, /device:TPU:1, one launch (start us, length us, event | category | flops | bytes accessed | tf_op | source)
XLA Modules:
  0.0 71.9 jit_solution(13472731264634027006)
XLA Ops:
  0.6 0.7 copy.15
  1.3 0.8 %copy.12.sends = s32[5,2]{1,0:T(8,128)S(1)} copy(s32[5,2]{0,1:T(2,128)} %bitcast.22) | data formatting | bytes 80 | tf_op jit(solution)/shard_map/squeeze | solution.py:441
  2.1 0.8 %copy.11.kernel_points = f32[15,3]{1,0:T(8,128)S(1)} copy(f32[15,3]{0,1:T(4,128)} %param.10) | data formatting | bytes 360 | tf_op args[2]
  2.9 0.0 copy-start
  2.9 1.5 %copy-done = bf16[3840,256]{1,0:T(8,128)(2,1)S(1)} copy-done((bf16[3840,256]{1,0:T(8,128)(2,1)S(1)}, bf16[3840,256]{1,0:T(8,128)(2,1)}, u32[]{:S(2)}) %copy-start) | copy-done | bytes 1966104
  4.4 0.0 copy-start.1
  4.4 1.0 %copy-done.1 = s32[1,4,4,64,64]{4,3,2,1,0:T(8,128)S(1)} copy-done((s32[1,4,4,64,64]{4,3,2,1,0:T(8,128)S(1)}, s32[1,4,4,64,64]{4,3,2,1,0:T(8,128)}, u32[]{:S(2)}) %copy-start.1) | copy-done | bytes 262168
  5.4 0.0 copy-start.2
  5.4 0.9 %copy-done.2 = bf16[1,4,64,256]{3,2,1,0:T(8,128)(2,1)S(1)} copy-done((bf16[1,4,64,256]{3,2,1,0:T(8,128)(2,1)S(1)}, bf16[1,4,64,256]{3,2,1,0:T(8,128)(2,1)}, u32[]{:S(2)}) %copy-start.2) | copy-done | bytes 131096
  6.3 0.0 copy-start.3
  6.3 0.9 %copy-done.3 = bf16[1,4,64,256]{3,2,1,0:T(8,128)(2,1)S(1)} copy-done((bf16[1,4,64,256]{3,2,1,0:T(8,128)(2,1)S(1)}, bf16[1,4,64,256]{3,2,1,0:T(8,128)(2,1)}, u32[]{:S(2)}) %copy-start.3) | copy-done | bytes 131096
  7.2 0.0 copy-start.4
  7.3 0.7 copy-done.4
  7.9 60.3 %convolution.1 = (bf16[4,64,256]{2,1,0:T(8,128)(2,1)S(1)}, bf16[4,64,256]{2,1,0:T(8,128)(2,1)S(1)}, bf16[15,256,256]{2,1,0:T(8,128)(2,1)S(1)}) custom-call(bf16[4,64,256]{2,1,0:T(8,128)(2,1)S(1)} %bitcast.16, s32[3,256]{1,0:T(4,128)S(1)} %bitcast.20, f32[15,3]{1,0:T(8,128)S(1)} %copy.11.kernel_points, bf16[15,256,256]{2,1,0:T(8,128)(2,1)S(1)} %bitcast.14, ...), custom_call_target="tpu_custom_call" | custom-call | tf_op jit(solution)/shard_map/convolution/pallas_call | solution.py:394
  68.3 2.4 %bitcast_convert_fusion = f32[3840,256]{1,0:T(8,128)} fusion(bf16[15,256,256]{2,1,0:T(8,128)(2,1)S(1)} %get-tuple-element.8), kind=kLoop, calls=%fused_computation | loop fusion | flops 983040 | bytes 5898240 | tf_op jit(solution)/shard_map/reshape | solution.py:443
  70.6 0.7 copy.18
  71.3 0.7 copy.19
Async XLA Ops:
  2.9 1.5 %copy-start = (bf16[3840,256]{1,0:T(8,128)(2,1)S(1)}, bf16[3840,256]{1,0:T(8,128)(2,1)}, u32[]{:S(2)}) copy-start(bf16[3840,256]{1,0:T(8,128)(2,1)} %param.11) | copy-start | bytes 5898244
  4.4 1.0 %copy-start.1 = (s32[1,4,4,64,64]{4,3,2,1,0:T(8,128)S(1)}, s32[1,4,4,64,64]{4,3,2,1,0:T(8,128)}, u32[]{:S(2)}) copy-start(s32[1,4,4,64,64]{4,3,2,1,0:T(8,128)} %param.13) | copy-start | bytes 786436
  5.4 0.9 %copy-start.2 = (bf16[1,4,64,256]{3,2,1,0:T(8,128)(2,1)S(1)}, bf16[1,4,64,256]{3,2,1,0:T(8,128)(2,1)}, u32[]{:S(2)}) copy-start(bf16[1,4,64,256]{3,2,1,0:T(8,128)(2,1)} %param.8) | copy-start | bytes 393220
  6.3 0.9 %copy-start.3 = (bf16[1,4,64,256]{3,2,1,0:T(8,128)(2,1)S(1)}, bf16[1,4,64,256]{3,2,1,0:T(8,128)(2,1)}, u32[]{:S(2)}) copy-start(bf16[1,4,64,256]{3,2,1,0:T(8,128)(2,1)} %param.15) | copy-start | bytes 393220
  7.2 0.7 copy-start.4

commit v3 on v2

--- a/solution.py
+++ b/solution.py
@@ -32,8 +32,12 @@
     return lambda: pl.semaphore_wait(barrier, len(others))
 
 
+def steps_of(count):
+    return sorted(range(1, count), key=lambda step: -min(step, count - step))
+
+
 def around(position, count):
-    return [lax.rem(position + step, count) for step in range(1, count)]
+    return [lax.rem(position + step, count) for step in steps_of(count)]
 
 
 def product(left, right, dims):
@@ -42,21 +46,21 @@
 
 def copy_counts(nx, nz, kernels, rounds):
     chunks = -(-kernels // CHUNK)
-    return 3 * rounds + 1 + chunks * (2 + 4 * (nx - 1) + 4 * (NY - 1) + 2 * (nz - 1))
+    return 3 * rounds + 1 + chunks * (2 + 4 * (nx - 1) + 4 * (NY - 1) + 2 * (nz - 1) + nx + NY)
 
 
 def kernel(
     nx, nz, kernels, rounds,
-    feats, coords, kernel_points, weights_hbm, slots, mask_hbm, sends, cot,
+    feats_in, coords_in, kernel_points_in, weights_in, slots_in, mask_in, sends_in, cot_in,
     output, grad, final,
-    weights, mask, pool_feats, pool_pos, own_pos, send_feats, send_pos, query, cot_pair, h, grad_summed, grad_support,
-    send_grad, got_grad, support, summed, summed_pair, out_sum, partial, got_first, part, got_second,
+    feats, coords, kernel_points, weights, slots, mask, sends, cot, pool_feats, pool_pos, own_pos, send_feats, send_pos, query, cot_pair, h, grad_summed, grad_support,
+    send_grad, got_grad, support, summed, summed_pair, partial, got_first, part, got_second,
     slab, got_z, piece, gather_z, gather_second,
     local_sem, send_sem, recv_sem,
 ):
     leaves, points, channels = feats.shape
     near = slots.shape[1]
-    bound = sends.shape[1]
+    bound = sends.shape[0]
     x, y, z, core = place()
     dom = z * NY + y
     sibling = device(x, y, z, 1 - core)
@@ -79,10 +83,14 @@
         others += [to(o) for o in around(at, count)]
     all_here = greet(others)
 
-    load_weights = pltpu.make_async_copy(weights_hbm, weights, local_sem.at[0])
-    load_weights.start()
-    load_mask = pltpu.make_async_copy(mask_hbm, mask, local_sem.at[1])
-    load_mask.start()
+    loads = {}
+    for index, (name, src, dst) in enumerate((
+        ("sends", sends_in, sends), ("coords", coords_in, coords), ("feats", feats_in, feats),
+        ("cot", cot_in, cot), ("slots", slots_in, slots), ("points", kernel_points_in, kernel_points),
+        ("weights", weights_in, weights), ("mask", mask_in, mask),
+    )):
+        loads[name] = pltpu.make_async_copy(src, dst, local_sem.at[index])
+        loads[name].start()
 
     number = [0]
     started = []
@@ -102,7 +110,9 @@
         for copy in copies:
             copy.wait_recv()
 
-    positions = coords[...].astype(F32) * QUANT
+    for name in ("sends", "coords", "feats"):
+        loads[name].wait()
+    positions = coords[...].reshape(3, leaves * points).astype(F32) * QUANT
     for leaf in range(leaves):
         own = positions[:, leaf * points : (leaf + 1) * points]
         both = jnp.concatenate([own, own], 1)
@@ -111,7 +121,7 @@
         pool_feats[leaf] = feats[leaf]
     for bit in range(rounds):
         for t in range(bound):
-            chosen = sends[bit, t]
+            chosen = sends[t, bit]
             send_feats[bit * bound + t] = feats[chosen]
             send_pos[bit * bound + t] = own_pos[chosen]
     all_here()
@@ -122,6 +132,7 @@
     for bit in reversed(range(rounds)):
         entry, there = pl.ds(bit * bound, bound), pl.ds(leaves + bit * bound, bound)
         copies_feats.append(push(send_feats.at[entry], pool_feats.at[there], partners[bit]))
+    loads["cot"].wait()
     copy_cot = push(cot, cot_pair, sibling)
 
     rows = lax.broadcasted_iota(jnp.int32, (points, 2 * points), 0)
@@ -131,18 +142,16 @@
             line = jnp.where(rows == lanes, pool_pos[leaf, c : c + 1, :], 0.0)
             query[c, leaf] = jnp.broadcast_to(jnp.sum(line, 1, keepdims=True), (points, 2 * points))
 
-    load_weights.wait()
-
-    def grads(k, _):
-        block = product(cot[...].reshape(leaves * points, channels), weights[k], ((1,), (1,)))
+    loads["weights"].wait()
+
+    upstream = cot[...].reshape(leaves * points, channels)
+    for k in range(kernels):
+        block = product(upstream, weights[k], ((1,), (1,)))
         grad_summed[:, k] = block.astype(BF16).reshape(leaves, points, channels)
-        return 0
-
-    lax.fori_loop(0, kernels, grads, 0)
-
-    load_mask.wait()
+
+    for name in ("slots", "points", "mask"):
+        loads[name].wait()
     arrive(copies_pos)
-    unroll = 3 if kernels % 3 == 0 else 1
 
     def correlate(leaf, _):
         for pair in range(near // 2):
@@ -153,28 +162,72 @@
             apart = [places[c : c + 1, :] - query[c, leaf] for c in range(3)]
             shown = jnp.concatenate([mask[leaf, 2 * pair], mask[leaf, 2 * pair + 1]], 1).astype(F32)
 
-            def one(step, _):
-                for k in [step * unroll + u for u in range(unroll)]:
-                    squared = jnp.full(shown.shape, EPSILON, F32)
-                    for c in range(3):
-                        difference = apart[c] - kernel_points[k, c]
-                        squared = squared + difference * difference
-                    weight = jnp.maximum(1.0 - squared * lax.rsqrt(squared), 0.0) * shown
-                    h[leaf, k, :, pair * 2 * points : (pair + 1) * 2 * points] = weight.astype(BF16)
-                return 0
-
-            lax.fori_loop(0, kernels // unroll, one, 0)
+            for k in range(kernels):
+                squared = jnp.full(shown.shape, EPSILON, F32)
+                for c in range(3):
+                    difference = apart[c] - kernel_points[c, k]
+                    squared = squared + difference * difference
+                weight = jnp.maximum(1.0 - squared * lax.rsqrt(squared), 0.0) * shown
+                h[leaf, k, :, pair * 2 * points : (pair + 1) * 2 * points] = weight.astype(BF16)
         return 0
 
     lax.fori_loop(0, leaves, correlate, 0)
 
-    def supports(leaf, _):
+    half = channels // CORES
+    own_half = pl.ds(pl.multiple_of(core * half, half), half)
+    pair_half = pl.ds(pl.multiple_of((1 - core) * half, half), half)
+    chunks = [(k0, min(CHUNK, kernels - k0)) for k0 in range(0, kernels, CHUNK)]
+    groups = []
+    for k0, nk in chunks:
+        cut = min(CHUNK // 2, nk)
+        groups.append([(k0, cut, "x", "y"), (k0 + cut, nk - cut, "y", "x")])
+    arrive(copies_feats)
+    for leaf in range(leaves):
+        for n in range(near):
+            support[leaf, n * points : (n + 1) * points, :] = pool_feats[slots[leaf, n]]
+    copies_summed = []
+    for g0, ng, _, _ in sum(groups, []):
+        for leaf in range(leaves):
+            left = h[leaf, g0 : g0 + ng].reshape(ng * points, near * points)
+            block = product(left, support[leaf], ((1,), (0,))).astype(BF16)
+            summed[g0 : g0 + ng, leaf * points : (leaf + 1) * points, :] = block.reshape(ng, points, channels)
+        there = pl.ds(g0, ng)
+        copies_summed.append(push(summed.at[there, :, pair_half], summed_pair.at[there], sibling))
+
+    for leaf in range(leaves):
         left = h[leaf].reshape(kernels * points, near * points)
         right = grad_summed[leaf].reshape(kernels * points, channels)
         grad_support[leaf] = product(left, right, ((0,), (0,)))
-        return 0
-
-    lax.fori_loop(0, leaves, supports, 0)
+
+    arrive([copy_cot])
+
+    def band(axis, at):
+        block = half // axes[axis][1]
+        return pl.ds(pl.multiple_of(at * block, block), block)
+
+    def tile(axis, at):
+        block = part.shape[1] // (axes[axis][1] // 2)
+        width = channels // 2
+        down, across = at // 2, lax.rem(at, 2)
+        return pl.ds(pl.multiple_of(down * block, block), block), pl.ds(pl.multiple_of(across * width, width), width)
+
+    upstream_pair = cot_pair[...].reshape(leaves * points, channels)
+    firsts = []
+    for pieces in groups:
+        sent = []
+        for g0, ng, first, _ in pieces:
+            arrive([copies_summed.pop(0)])
+            for k in range(g0, g0 + ng):
+                block = product(summed[k, :, own_half].T, upstream, ((1,), (0,)))
+                block += product(summed_pair[k].T, upstream_pair, ((1,), (0,)))
+                partial[k] = block.astype(BF16)
+            there = pl.ds(g0, ng)
+            at, count, to = axes[first]
+            sent.append([
+                push(partial.at[there, band(first, o), :], got_first.at[step, there], to(o))
+                for step, o in enumerate(around(at, count))
+            ])
+        firsts.append(sent)
 
     def gathered(entry, total):
         for leaf in range(leaves):
@@ -189,78 +242,18 @@
 
     lax.fori_loop(0, rounds * bound, away, 0)
     copies_grad = []
-    for bit in reversed(range(rounds)):
-        entry = pl.ds(bit * bound, bound)
-        copies_grad.append(push(send_grad.at[entry], got_grad.at[entry], partners[bit]))
-
-    half = channels // CORES
-    own_half = pl.ds(pl.multiple_of(core * half, half), half)
-    pair_half = pl.ds(pl.multiple_of((1 - core) * half, half), half)
-    chunks = [(k0, min(CHUNK, kernels - k0)) for k0 in range(0, kernels, CHUNK)]
-    arrive(copies_feats)
-    for leaf in range(leaves):
-        for n in range(near):
-            support[leaf, n * points : (n + 1) * points, :] = pool_feats[slots[leaf, n]]
-    copies_summed = []
-    for k0, nk in chunks:
-
-        def sums(leaf, _, k0=k0, nk=nk):
-            left = h[leaf, k0 : k0 + nk].reshape(nk * points, near * points)
-            block = product(left, support[leaf], ((1,), (0,))).astype(BF16)
-            at = pl.ds(pl.multiple_of(leaf * points, points), points)
-            summed[k0 : k0 + nk, at, :] = block.reshape(nk, points, channels)
-            return 0
-
-        lax.fori_loop(0, leaves, sums, 0)
-        there = pl.ds(k0, nk)
-        copies_summed.append(push(summed.at[there, :, pair_half], summed_pair.at[there], sibling))
-
-    arrive([copy_cot])
-    groups = []
-    for k0, nk in chunks:
-        cut = min(CHUNK // 2, nk)
-        groups.append([(k0, cut, "x", "y"), (k0 + cut, nk - cut, "y", "x")])
-
-    def band(axis, at):
-        block = half // axes[axis][1]
-        return pl.ds(pl.multiple_of(at * block, block), block)
-
-    def tile(axis, at):
-        block = part.shape[1] // (axes[axis][1] // 2)
-        width = channels // 2
-        down, across = at // 2, lax.rem(at, 2)
-        return pl.ds(pl.multiple_of(down * block, block), block), pl.ds(pl.multiple_of(across * width, width), width)
-
-    firsts = []
-    for (k0, nk), copy, pieces in zip(chunks, copies_summed, groups):
-        arrive([copy])
-
-        def terms(k, _):
-            block = product(summed[k, :, own_half], cot[...].reshape(leaves * points, channels), ((0,), (0,)))
-            block += product(summed_pair[k], cot_pair[...].reshape(leaves * points, channels), ((0,), (0,)))
-            partial[k] = block.astype(BF16)
-            return 0
-
-        sent = []
-        for g0, ng, first, _ in pieces:
-            lax.fori_loop(g0, g0 + ng, terms, 0)
-            at, count, to = axes[first]
-            there = pl.ds(g0, ng)
-            sent.append([
-                push(partial.at[there, band(first, o), :], got_first.at[step, there], to(o))
-                for step, o in enumerate(around(at, count))
-            ])
-        firsts.append(sent)
-
-    out_sum[...] = jnp.zeros(out_sum.shape, F32)
-
-    def outputs(k, _):
-        out_sum[...] += product(summed[k], weights[k], ((1,), (0,)))
-        return 0
-
-    lax.fori_loop(0, kernels, outputs, 0)
-    output[...] = out_sum[...].astype(BF16).reshape(output.shape)
-
+
+    def hand_back(bits):
+        for bit in reversed(bits):
+            entry = pl.ds(bit * bound, bound)
+            copies_grad.append(push(send_grad.at[entry], got_grad.at[entry], partners[bit]))
+
+    hand_back(range(low, rounds))
+
+    total = product(summed[0], weights[0], ((1,), (0,)))
+    for k in range(1, kernels):
+        total = total + product(summed[k], weights[k], ((1,), (0,)))
+    output[...] = total.astype(BF16).reshape(output.shape)
     seconds = []
     for sent, pieces in zip(firsts, groups):
         again = []
@@ -285,18 +278,7 @@
             ])
         seconds.append(again)
 
-    arrive(copies_grad)
-
-    def owned(leaf, _):
-        total = gathered(leaf, grad_support[leaf, 0:points, :])
-        for bit in range(rounds):
-            for t in range(bound):
-                named = jnp.where(sends[bit, t] == leaf, 1.0, 0.0)
-                total = total + named * got_grad[bit * bound + t].astype(F32)
-        grad[leaf] = total.astype(BF16)
-        return 0
-
-    lax.fori_loop(0, leaves, owned, 0)
+    hand_back(range(low))
 
     per_z = CHUNK // nz
     for k in range(kernels, slab.shape[0]):
@@ -332,6 +314,19 @@
         piece[index] = (total / (nx * NY * nz * CORES)).astype(BF16)
         back_z.append([push(piece.at[index], gather_z.at[own], to(o)) for o in around(at, count)])
         gather_z[own] = piece[index]
+    arrive(copies_grad)
+
+    def owned(leaf, _):
+        total = gathered(leaf, grad_support[leaf, 0:points, :])
+        for bit in range(rounds):
+            for t in range(bound):
+                named = jnp.where(sends[t, bit] == leaf, 1.0, 0.0)
+                total = total + named * got_grad[bit * bound + t].astype(F32)
+        grad[leaf] = total.astype(BF16)
+        return 0
+
+    lax.fori_loop(0, leaves, owned, 0)
+
     back_second = []
     for copies, pieces in zip(back_z, groups):
         arrive(copies)
@@ -346,28 +341,47 @@
             gather_second[there, own[0], own[1]] = gather_z[there]
         back_second.append(sent)
     back_first = []
+    lasts = []
+
+    def front(first, at):
+        block = half // axes[first][1]
+        return pl.ds(pl.multiple_of(core * half + at * block, block), block)
+
+    def share(there, own):
+        lasts.append(push(final.at[there, own, :], final.at[there, own, :], sibling))
+
     for sent, pieces in zip(back_second, groups):
-        again = []
         for copies, (g0, ng, first, _) in zip(sent, pieces):
             arrive(copies)
             at, count, to = axes[first]
             there = pl.ds(g0, ng)
-            block = half // count
-            own = pl.ds(pl.multiple_of(core * half + at * block, block), block)
-            again.append([
+            own = front(first, at)
+            back_first.append([
                 push(gather_second.at[there], final.at[there, own, :], to(o)) for o in around(at, count)
             ])
             final[there, own, :] = gather_second[there]
-        back_first.append(again)
-    lasts = []
-    for again, (k0, nk) in zip(back_first, chunks):
-        for copies in again:
-            arrive(copies)
-        mine = final.at[pl.ds(k0, nk), own_half, :]
-        lasts.append(push(mine, mine, sibling))
+            share(there, own)
+    for copies, (g0, ng, first, _) in zip(back_first, sum(groups, [])):
+        at, count, _ = axes[first]
+        for copy, step in reversed(list(zip(copies, steps_of(count)))):
+            arrive([copy])
+            share(pl.ds(g0, ng), front(first, lax.rem(at + count - step, count)))
     arrive(lasts)
     for copy in started:
         copy.wait_send()
+
+
+def write_kernel(output, grad, mean, output_out, grad_out, mean_out, wide, sem):
+    copies = []
+    for index, (src, dst) in enumerate(((output, output_out), (grad, grad_out))):
+        copies.append(pltpu.make_async_copy(src, dst, sem.at[index]))
+        copies[-1].start()
+    for k in range(mean.shape[0]):
+        wide[k] = mean[k].astype(F32)
+        copies.append(pltpu.make_async_copy(wide.at[k], mean_out.at[k], sem.at[2 + k]))
+        copies[-1].start()
+    for copy in copies:
+        copy.wait()
 
 
 def shards(features, coords, kernel_points, weights, support_slot, slot_mask, send_leaf, cotangent):
@@ -386,9 +400,7 @@
     tile = band // (wide // 2)
     width = channels // 2
     copies = copy_counts(nx, nz, kernels, rounds)
-    vmem, smem, anywhere = (
-        pl.BlockSpec(memory_space=space) for space in (pltpu.VMEM, pltpu.SMEM, pl.ANY)
-    )
+    vmem, hbm = (pl.BlockSpec(memory_space=space) for space in (pltpu.VMEM, pltpu.HBM))
     cube = (kernels, channels, channels)
     leaf_shape = (leaves, points, channels)
     output, grad, mean = pl.pallas_call(
@@ -398,11 +410,17 @@
             jax.ShapeDtypeStruct(leaf_shape, BF16),
             jax.ShapeDtypeStruct(cube, BF16),
         ),
-        in_specs=[vmem, vmem, smem, anywhere, smem, anywhere, smem, vmem],
+        in_specs=[hbm] * 8,
         out_specs=(vmem, vmem, vmem),
         scratch_shapes=[
+            pltpu.VMEM(leaf_shape, BF16),
+            pltpu.VMEM((3, 1, leaves * points), jnp.int32),
+            pltpu.SMEM((3, kernels), F32),
             pltpu.VMEM(cube, BF16),
+            pltpu.SMEM((leaves, near), jnp.int32),
             pltpu.VMEM(slot_mask.shape[1:], jnp.int32),
+            pltpu.SMEM((bound, rounds), jnp.int32),
+            pltpu.VMEM(leaf_shape, BF16),
             pltpu.VMEM((leaves + received, points, channels), BF16),
             pltpu.VMEM((leaves + received, 8, 2 * points), F32),
             pltpu.VMEM((leaves, 8, 2 * points), F32),
@@ -418,7 +436,6 @@
             pltpu.VMEM((leaves, near * points, channels), BF16),
             pltpu.VMEM((kernels, leaves * points, channels), BF16),
             pltpu.VMEM((kernels, leaves * points, half), BF16),
-            pltpu.VMEM((leaves * points, channels), F32),
             pltpu.VMEM((kernels, half, channels), BF16),
             pltpu.VMEM((wide - 1, kernels, band, channels), BF16),
             pltpu.VMEM((kernels, band, channels), BF16),
@@ -428,7 +445,7 @@
             pltpu.VMEM((chunks, CHUNK // nz, tile, width), BF16),
             pltpu.VMEM((padded, tile, width), BF16),
             pltpu.VMEM((kernels, band, channels), BF16),
-            pltpu.SemaphoreType.DMA((2,)),
+            pltpu.SemaphoreType.DMA((8,)),
             pltpu.SemaphoreType.DMA((copies,)),
             pltpu.SemaphoreType.DMA((copies,)),
         ],
@@ -437,11 +454,28 @@
         ),
         name="convolution",
     )(
-        features[0], coords[0], kernel_points, weights.reshape(cube), support_slot[0], slot_mask[0],
-        send_leaf[0, 0], cotangent[0],
+        *(
+            pltpu.with_memory_space_constraint(operand, pltpu.HBM)
+            for operand in (
+                features[0], coords.transpose(1, 0, 2), kernel_points.T, weights.reshape(cube), support_slot[0],
+                slot_mask[0], send_leaf[0, 0].T, cotangent[0],
+            )
+        )
     )
-    grad_weight = mean.astype(F32).reshape(kernels * channels, channels)
-    return (output[None], grad[None], grad_weight)
+    output, grad, grad_weight = pl.pallas_call(
+        write_kernel,
+        out_shape=(
+            jax.ShapeDtypeStruct(leaf_shape, BF16),
+            jax.ShapeDtypeStruct(leaf_shape, BF16),
+            jax.ShapeDtypeStruct(cube, F32),
+        ),
+        in_specs=[vmem, vmem, vmem],
+        out_specs=(hbm, hbm, hbm),
+        scratch_shapes=[pltpu.VMEM(cube, F32), pltpu.SemaphoreType.DMA((2 + kernels,))],
+        compiler_params=pltpu.CompilerParams(vmem_limit_bytes=16 * 1024 * 1024),
+        name="write",
+    )(output, grad, mean)
+    return (output[None], grad[None], grad_weight.reshape(kernels * channels, channels))
 
 
 def solution(mesh):

time: 72.2 us -> 57.4 us (0.80)
  local copies, waits for them, and re-layouts: 8.6 us -> 0 us
  Pallas kernels: 60.3 us -> 56.7 us
  other arithmetic: 2.36 us -> 0 us
    unnamed x14 -> x0, local copies, waits for them, and re-layouts: 7.84 us -> none
    pallas_call x1, Pallas kernels: 60.3 us -> 54.5 us  [shards(): pl.pallas_call(functools.partial(kernel, nx, nz, kernels, rounds), out_sh...]
    reshape x1 -> x0, other arithmetic: 2.36 us -> none  [shards(): grad_weight = mean.astype(F32).reshape(kernels * channels, channels)]
    pallas_call x0 -> x1, Pallas kernels: none -> 2.14 us  [shards(): pl.pallas_call(write_kernel, out_shape=(jax.ShapeDtypeStruct(leaf_shape,...]
    squeeze x1 -> x0, local copies, waits for them, and re-layouts: 0.76 us -> none  [shards(): send_leaf[0, 0]]
where the time goes in v3:
time: 57.4 us; the launch traced here: 57.3 us
  Pallas kernels  56.7 us (99%)
  between operations  0.64 us (1%)
    pallas_call x1, Pallas kernels, shards(): pl.pallas_call(functools.partial(kernel, nx, nz, kernels, rounds), out_sh...  54.5 us
    pallas_call x1, Pallas kernels, shards(): pl.pallas_call(write_kernel, out_shape=(jax.ShapeDtypeStruct(leaf_shape,...  2.14 us

profile of v3, /device:TPU:1, one launch (start us, length us, event | category | flops | bytes accessed | tf_op | source)
XLA Modules:
  0.0 57.3 jit_solution(5353965183284376350)
XLA Ops:
  0.6 54.5 %convolution.1 = (bf16[4,64,256]{2,1,0:T(8,128)(2,1)S(1)}, bf16[4,64,256]{2,1,0:T(8,128)(2,1)S(1)}, bf16[15,256,256]{2,1,0:T(8,128)(2,1)S(1)}) custom-call(bf16[4,64,256]{2,1,0:T(8,128)(2,1)} %bitcast.15, s32[3,1,256]{2,1,0:T(1,128)} %bitcast.17, f32[3,15]{1,0:T(4,128)} %bitcast.18, bf16[15,256,256]{2,1,0:T(8,128)(2,1)} %bitcast.13, s32[4,4]{1,0:T(4,128)} %bitcast.19, ...), custom_call_target="tpu_custom_call" | custom-call | tf_op jit(solution)/shard_map/convolution/pallas_call | solution.py:406
  55.2 2.1 %write.1 = (bf16[4,64,256]{2,1,0:T(8,128)(2,1)}, bf16[4,64,256]{2,1,0:T(8,128)(2,1)}, f32[15,256,256]{2,1,0:T(8,128)}) custom-call(bf16[4,64,256]{2,1,0:T(8,128)(2,1)S(1)} %get-tuple-element.9.output, bf16[4,64,256]{2,1,0:T(8,128)(2,1)S(1)} %get-tuple-element.10.grad, bf16[15,256,256]{2,1,0:T(8,128)(2,1)S(1)} %get-tuple-element.11.mean), custom_call_target="tpu_custom_call" | custom-call | tf_op jit(solution)/shard_map/write/pallas_call | solution.py:465

commit v4 on v3

--- a/solution.py
+++ b/solution.py
@@ -12,6 +12,7 @@
 CORES = 2
 NY = 4
 CHUNK = 8
+CHUNKS = 2
 MESH = pl.DeviceIdType.MESH
 F32, BF16 = jnp.float32, jnp.bfloat16
 
@@ -29,7 +30,10 @@
     barrier = pltpu.get_barrier_semaphore()
     for other in others:
         pl.semaphore_signal(barrier, inc=1, device_id=other, device_id_type=MESH)
-    return lambda: pl.semaphore_wait(barrier, len(others))
+
+
+def all_here(count):
+    pl.semaphore_wait(pltpu.get_barrier_semaphore(), count)
 
 
 def steps_of(count):
@@ -44,9 +48,8 @@
     return lax.dot_general(left, right, (dims, ((), ())), preferred_element_type=F32)
 
 
-def copy_counts(nx, nz, kernels, rounds):
-    chunks = -(-kernels // CHUNK)
-    return 3 * rounds + 1 + chunks * (2 + 4 * (nx - 1) + 4 * (NY - 1) + 2 * (nz - 1) + nx + NY)
+def copy_counts(nx, nz, rounds):
+    return 3 * rounds + 1 + CHUNKS * (2 + 6 * (nx - 1 + NY - 1) + 4 + 2 * (nz - 1) + nx + NY)
 
 
 def kernel(
@@ -54,7 +57,7 @@
     feats_in, coords_in, kernel_points_in, weights_in, slots_in, mask_in, sends_in, cot_in,
     output, grad, final,
     feats, coords, kernel_points, weights, slots, mask, sends, cot, pool_feats, pool_pos, own_pos, send_feats, send_pos, query, cot_pair, h, grad_summed, grad_support,
-    send_grad, got_grad, support, summed, summed_pair, partial, got_first, part, got_second,
+    send_grad, got_grad, support, summed, summed_pair, partial, partial_pair, got_first, part, got_second,
     slab, got_z, piece, gather_z, gather_second,
     local_sem, send_sem, recv_sem,
 ):
@@ -65,9 +68,9 @@
     dom = z * NY + y
     sibling = device(x, y, z, 1 - core)
     axes = {
-        "x": (x, nx, lambda o: device(o, y, z, core)),
-        "y": (y, NY, lambda o: device(x, o, z, core)),
-        "z": (z, nz, lambda o: device(x, y, o, core)),
+        "x": (x, nx, lambda o, c: device(o, y, z, c)),
+        "y": (y, NY, lambda o, c: device(x, o, z, c)),
+        "z": (z, nz, lambda o, c: device(x, y, o, c)),
     }
     low = NY.bit_length() - 1
     partners = []
@@ -78,10 +81,16 @@
         else:
             side = 1 << (bit - low)
             partners.append(device(x, y, z + side - 2 * side * lax.rem(z // side, 2), core))
-    others = [sibling]
-    for at, count, to in axes.values():
-        others += [to(o) for o in around(at, count)]
-    all_here = greet(others)
+    rings = {axis: [(to, o) for o in around(at, count)] for axis, (at, count, to) in axes.items()}
+    plane = rings["x"] + rings["y"]
+
+    @pl.when(core == 1)
+    def _():
+        greet([sibling] + [to(o, 1) for to, o in plane + rings["z"]] + [to(o, 0) for to, o in plane])
+
+    @pl.when(core == 0)
+    def _():
+        greet([sibling] + partners + [to(o, 1) for to, o in plane])
 
     loads = {}
     for index, (name, src, dst) in enumerate((
@@ -94,14 +103,20 @@
 
     number = [0]
     started = []
-
-    def push(src, dst, other):
+    settled = [0]
+
+    def describe(src, dst, other):
         index = number[0]
         number[0] += 1
-        copy = pltpu.make_async_remote_copy(
+        return pltpu.make_async_remote_copy(
             src_ref=src, dst_ref=dst, send_sem=send_sem.at[index], recv_sem=recv_sem.at[index],
             device_id=other, device_id_type=MESH,
         )
+
+    def push(src, dst, other):
+        return begin(describe(src, dst, other))
+
+    def begin(copy):
         copy.start()
         started.append(copy)
         return copy
@@ -109,6 +124,11 @@
     def arrive(copies):
         for copy in copies:
             copy.wait_recv()
+
+    def settle(count):
+        for copy in started[settled[0] : count]:
+            copy.wait_send()
+        settled[0] = max(settled[0], count)
 
     for name in ("sends", "coords", "feats"):
         loads[name].wait()
@@ -124,7 +144,15 @@
             chosen = sends[t, bit]
             send_feats[bit * bound + t] = feats[chosen]
             send_pos[bit * bound + t] = own_pos[chosen]
-    all_here()
+
+    @pl.when(core == 1)
+    def _():
+        all_here(1 + 2 * len(plane) + len(rings["z"]))
+
+    @pl.when(core == 0)
+    def _():
+        all_here(1 + len(partners) + len(plane))
+
     copies_pos, copies_feats = [], []
     for bit in reversed(range(rounds)):
         entry, there = pl.ds(bit * bound, bound), pl.ds(leaves + bit * bound, bound)
@@ -176,17 +204,49 @@
     half = channels // CORES
     own_half = pl.ds(pl.multiple_of(core * half, half), half)
     pair_half = pl.ds(pl.multiple_of((1 - core) * half, half), half)
-    chunks = [(k0, min(CHUNK, kernels - k0)) for k0 in range(0, kernels, CHUNK)]
+    chunks = [(kernels * i // CHUNKS, kernels * (i + 1) // CHUNKS - kernels * i // CHUNKS) for i in range(CHUNKS)]
     groups = []
     for k0, nk in chunks:
-        cut = min(CHUNK // 2, nk)
+        cut = (nk + 1) // 2
         groups.append([(k0, cut, "x", "y"), (k0 + cut, nk - cut, "y", "x")])
+    pairs = sum(groups, [])
+
+    def band(axis, at, start=0):
+        block = half // axes[axis][1]
+        return pl.ds(pl.multiple_of(start + at * block, block), block)
+
+    def tile(axis, at):
+        block = part.shape[1] // axes[axis][1]
+        return pl.ds(pl.multiple_of(at * block, block), block)
+
+    firsts, fronts, lasts = {}, {}, {}
+    for g0, ng, first, _ in pairs:
+        there = pl.ds(g0, ng)
+        at, count, to = axes[first]
+        block = half // count
+        for side in range(CORES):
+            rows = pl.ds(side * block, block)
+            for step, o in zip(steps_of(count), around(at, count)):
+                firsts[g0, step, side] = describe(
+                    partial.at[there, band(first, o), :], got_first.at[step - 1, there, rows, :], to(o, 1)
+                )
+                fronts[g0, step, side] = describe(
+                    gather_second.at[there, rows, :], final.at[there, band(first, at, side * half), :], to(o, side)
+                )
+        firsts[g0, 0, 0] = describe(partial.at[there, band(first, at), :], partial_pair.at[there], sibling)
+        fronts[g0, 0, 0] = describe(
+            gather_second.at[there, pl.ds(0, block), :], final.at[there, band(first, at), :], sibling
+        )
+        for step in range(count):
+            here = final.at[there, band(first, lax.rem(at + count - step, count), core * half), :]
+            lasts[g0, step] = describe(here, here, sibling)
+
     arrive(copies_feats)
     for leaf in range(leaves):
         for n in range(near):
             support[leaf, n * points : (n + 1) * points, :] = pool_feats[slots[leaf, n]]
     copies_summed = []
-    for g0, ng, _, _ in sum(groups, []):
+    for g0, ng, _, _ in pairs:
         for leaf in range(leaves):
             left = h[leaf, g0 : g0 + ng].reshape(ng * points, near * points)
             block = product(left, support[leaf], ((1,), (0,))).astype(BF16)
@@ -194,40 +254,20 @@
         there = pl.ds(g0, ng)
         copies_summed.append(push(summed.at[there, :, pair_half], summed_pair.at[there], sibling))
 
-    for leaf in range(leaves):
-        left = h[leaf].reshape(kernels * points, near * points)
-        right = grad_summed[leaf].reshape(kernels * points, channels)
-        grad_support[leaf] = product(left, right, ((0,), (0,)))
-
     arrive([copy_cot])
-
-    def band(axis, at):
-        block = half // axes[axis][1]
-        return pl.ds(pl.multiple_of(at * block, block), block)
-
-    def tile(axis, at):
-        block = part.shape[1] // (axes[axis][1] // 2)
-        width = channels // 2
-        down, across = at // 2, lax.rem(at, 2)
-        return pl.ds(pl.multiple_of(down * block, block), block), pl.ds(pl.multiple_of(across * width, width), width)
-
     upstream_pair = cot_pair[...].reshape(leaves * points, channels)
-    firsts = []
-    for pieces in groups:
-        sent = []
-        for g0, ng, first, _ in pieces:
-            arrive([copies_summed.pop(0)])
-            for k in range(g0, g0 + ng):
-                block = product(summed[k, :, own_half].T, upstream, ((1,), (0,)))
-                block += product(summed_pair[k].T, upstream_pair, ((1,), (0,)))
-                partial[k] = block.astype(BF16)
-            there = pl.ds(g0, ng)
-            at, count, to = axes[first]
-            sent.append([
-                push(partial.at[there, band(first, o), :], got_first.at[step, there], to(o))
-                for step, o in enumerate(around(at, count))
-            ])
-        firsts.append(sent)
+    for copy, (g0, ng, first, _) in zip(copies_summed, pairs):
+        arrive([copy])
+        for k in range(g0, g0 + ng):
+            block = product(summed[k, :, own_half].T, upstream, ((1,), (0,)))
+            block += product(summed_pair[k].T, upstream_pair, ((1,), (0,)))
+            partial[k] = block.astype(BF16)
+        for side in range(CORES):
+
+            @pl.when(core == side)
+            def _():
+                for step in steps_of(axes[first][1]) + [0] * (1 - side):
+                    firsts[g0, step, side].start()
 
     def gathered(entry, total):
         for leaf in range(leaves):
@@ -240,81 +280,25 @@
         send_grad[entry] = gathered(entry + leaves, jnp.zeros((points, channels), F32)).astype(BF16)
         return 0
 
-    lax.fori_loop(0, rounds * bound, away, 0)
-    copies_grad = []
+    def feature_gradients():
+        for leaf in range(leaves):
+            left = h[leaf].reshape(kernels * points, near * points)
+            right = grad_summed[leaf].reshape(kernels * points, channels)
+            grad_support[leaf] = product(left, right, ((0,), (0,)))
+        lax.fori_loop(0, rounds * bound, away, 0)
 
     def hand_back(bits):
+        copies = []
         for bit in reversed(bits):
             entry = pl.ds(bit * bound, bound)
-            copies_grad.append(push(send_grad.at[entry], got_grad.at[entry], partners[bit]))
-
-    hand_back(range(low, rounds))
-
-    total = product(summed[0], weights[0], ((1,), (0,)))
-    for k in range(1, kernels):
-        total = total + product(summed[k], weights[k], ((1,), (0,)))
-    output[...] = total.astype(BF16).reshape(output.shape)
-    seconds = []
-    for sent, pieces in zip(firsts, groups):
-        again = []
-        for copies, (g0, ng, first, second) in zip(sent, pieces):
-            arrive(copies)
-            at, count, _ = axes[first]
-            own = band(first, at)
-
-            def add_first(k, _, own=own, count=count):
-                total = partial[k, own, :].astype(F32)
-                for step in range(count - 1):
-                    total = total + got_first[step, k].astype(F32)
-                part[k] = total.astype(BF16)
-                return 0
-
-            lax.fori_loop(g0, g0 + ng, add_first, 0)
-            at, count, to = axes[second]
-            there = pl.ds(g0, ng)
-            again.append([
-                push(part.at[there, *tile(second, o)], got_second.at[step, there], to(o))
-                for step, o in enumerate(around(at, count))
-            ])
-        seconds.append(again)
-
-    hand_back(range(low))
-
-    per_z = CHUNK // nz
-    for k in range(kernels, slab.shape[0]):
-        slab[k] = jnp.zeros(slab.shape[1:], BF16)
-    thirds = []
-    for index, (again, pieces) in enumerate(zip(seconds, groups)):
-        for copies, (g0, ng, _, second) in zip(again, pieces):
-            arrive(copies)
-            at, count, _ = axes[second]
-            own = tile(second, at)
-
-            def add_second(k, _, own=own, count=count):
-                total = part[k, own[0], own[1]].astype(F32)
-                for step in range(count - 1):
-                    total = total + got_second[step, k].astype(F32)
-                slab[k] = total.astype(BF16)
-                return 0
-
-            lax.fori_loop(g0, g0 + ng, add_second, 0)
-        at, count, to = axes["z"]
-        thirds.append([
-            push(slab.at[pl.ds(index * CHUNK + o * per_z, per_z)], got_z.at[index, step], to(o))
-            for step, o in enumerate(around(at, count))
-        ])
-    back_z = []
-    for index, copies in enumerate(thirds):
-        arrive(copies)
-        at, count, to = axes["z"]
-        own = pl.ds(index * CHUNK + z * per_z, per_z)
-        total = slab[own].astype(F32)
-        for step in range(count - 1):
-            total = total + got_z[index, step].astype(F32)
-        piece[index] = (total / (nx * NY * nz * CORES)).astype(BF16)
-        back_z.append([push(piece.at[index], gather_z.at[own], to(o)) for o in around(at, count)])
-        gather_z[own] = piece[index]
-    arrive(copies_grad)
+            copies.append(push(send_grad.at[entry], got_grad.at[entry], partners[bit]))
+        return copies
+
+    def outputs():
+        total = product(summed[0], weights[0], ((1,), (0,)))
+        for k in range(1, kernels):
+            total = total + product(summed[k], weights[k], ((1,), (0,)))
+        output[...] = total.astype(BF16).reshape(output.shape)
 
     def owned(leaf, _):
         total = gathered(leaf, grad_support[leaf, 0:points, :])
@@ -325,50 +309,132 @@
         grad[leaf] = total.astype(BF16)
         return 0
 
-    lax.fori_loop(0, leaves, owned, 0)
-
-    back_second = []
-    for copies, pieces in zip(back_z, groups):
+    common = len(started), number[0]
+
+    def exchange(side):
+        for g0, ng, first, _ in pairs:
+            for step in steps_of(axes[first][1])[::-1]:
+                fronts[g0, step, side].wait_recv()
+                lasts[g0, step].start()
+            if side == 0:
+                fronts[g0, 0, 0].wait_recv()
+        for (_, step), copy in lasts.items():
+            if step > 0 or side == 0:
+                copy.wait_recv()
+        for (_, step), copy in lasts.items():
+            if step > 0 or side == 1:
+                copy.wait_send()
+
+    @pl.when(core == 0)
+    def _():
+        feature_gradients()
+        copies = hand_back(range(rounds))
+        outputs()
         arrive(copies)
-        sent = []
-        for g0, ng, _, second in pieces:
+        lax.fori_loop(0, leaves, owned, 0)
+        settle(len(started))
+        for (_, _, side), copy in firsts.items():
+            if side == 0:
+                copy.wait_send()
+        exchange(0)
+
+    del started[common[0] :]
+    number[0], settled[0] = common[1], 0
+
+    @pl.when(core == 1)
+    def _():
+        feature_gradients()
+        copies_grad = hand_back(range(low, rounds))
+        outputs()
+
+        seconds = {}
+        for g0, ng, first, second in pairs:
+            at, count, _ = axes[first]
+            block = half // count
+            for step in [0] + steps_of(count)[::-1]:
+                for side in range(CORES if step else 1):
+                    firsts[g0, step, side].wait_recv()
+            for k in range(g0, g0 + ng):
+                for side, own in ((0, partial_pair[k]), (1, partial[k, band(first, at), :])):
+                    rows = slice(side * block, (side + 1) * block)
+                    total = own.astype(F32)
+                    for step in range(count - 1):
+                        total = total + got_first[step, k, rows, :].astype(F32)
+                    part[k, rows, :] = total.astype(BF16)
             at, count, to = axes[second]
             there = pl.ds(g0, ng)
-            own = tile(second, at)
-            sent.append([
-                push(gather_z.at[there], gather_second.at[there, *own], to(o)) for o in around(at, count)
+            seconds[g0] = [
+                push(part.at[there, tile(second, o), :], got_second.at[step, there], to(o, 1))
+                for step, o in enumerate(around(at, count))
+            ]
+        copies_grad += hand_back(range(low))
+
+        per_z = CHUNK // nz
+        early = len(started)
+        thirds = []
+        for index, (k0, nk) in enumerate(chunks):
+            base = index * CHUNK - k0
+            for k in range(k0 + nk, k0 + CHUNK):
+                slab[base + k] = jnp.zeros(slab.shape[1:], BF16)
+            for g0, ng, _, second in groups[index]:
+                arrive(seconds[g0])
+                at, count, _ = axes[second]
+                for k in range(g0, g0 + ng):
+                    total = part[k, tile(second, at), :].astype(F32)
+                    for step in range(count - 1):
+                        total = total + got_second[step, k].astype(F32)
+                    slab[base + k] = total.astype(BF16)
+            at, count, to = axes["z"]
+            thirds.append([
+                push(slab.at[pl.ds(index * CHUNK + o * per_z, per_z)], got_z.at[index, step], to(o, 1))
+                for step, o in enumerate(around(at, count))
             ])
-            gather_second[there, own[0], own[1]] = gather_z[there]
-        back_second.append(sent)
-    back_first = []
-    lasts = []
-
-    def front(first, at):
-        block = half // axes[first][1]
-        return pl.ds(pl.multiple_of(core * half + at * block, block), block)
-
-    def share(there, own):
-        lasts.append(push(final.at[there, own, :], final.at[there, own, :], sibling))
-
-    for sent, pieces in zip(back_second, groups):
-        for copies, (g0, ng, first, _) in zip(sent, pieces):
+        devices = nx * NY * nz * CORES
+        back_z = []
+        for index, copies in enumerate(thirds):
             arrive(copies)
-            at, count, to = axes[first]
+            at, count, to = axes["z"]
+            own = pl.ds(index * CHUNK + z * per_z, per_z)
+            total = slab[own].astype(F32)
+            for step in range(count - 1):
+                total = total + got_z[index, step].astype(F32)
+            piece[index] = (total / devices).astype(BF16)
+            back_z.append([push(piece.at[index], gather_z.at[own], to(o, 1)) for o in around(at, count)])
+            gather_z[own] = piece[index]
+        arrive(copies_grad)
+        lax.fori_loop(0, leaves, owned, 0)
+        settle(early)
+
+        back_second = {}
+        for index, (k0, nk) in enumerate(chunks):
+            arrive(back_z[index])
+            for g0, ng, _, second in groups[index]:
+                at, count, to = axes[second]
+                there, here = pl.ds(g0, ng), pl.ds(index * CHUNK + g0 - k0, ng)
+                own = tile(second, at)
+                back_second[g0] = [
+                    push(gather_z.at[here], gather_second.at[there, own, :], to(o, 1)) for o in around(at, count)
+                ]
+                gather_second[there, own, :] = gather_z[here]
+        for g0, ng, first, _ in pairs:
+            arrive(back_second[g0])
+            at, count, _ = axes[first]
+            block = half // count
+            for step in steps_of(count) + [0]:
+                for side in range(CORES if step else 1):
+                    fronts[g0, step, side].start()
             there = pl.ds(g0, ng)
-            own = front(first, at)
-            back_first.append([
-                push(gather_second.at[there], final.at[there, own, :], to(o)) for o in around(at, count)
-            ])
-            final[there, own, :] = gather_second[there]
-            share(there, own)
-    for copies, (g0, ng, first, _) in zip(back_first, sum(groups, [])):
-        at, count, _ = axes[first]
-        for copy, step in reversed(list(zip(copies, steps_of(count)))):
-            arrive([copy])
-            share(pl.ds(g0, ng), front(first, lax.rem(at + count - step, count)))
-    arrive(lasts)
-    for copy in started:
-        copy.wait_send()
+            for side in range(CORES):
+                rows = slice(side * block, (side + 1) * block)
+                final[there, band(first, at, side * half), :] = gather_second[there, rows, :]
+            lasts[g0, 0].start()
+        settle(len(started))
+        for (_, _, side), copy in firsts.items():
+            if side == 1:
+                copy.wait_send()
+        exchange(1)
+        for copy in fronts.values():
+            copy.wait_send()
 
 
 def write_kernel(output, grad, mean, output_out, grad_out, mean_out, wide, sem):
@@ -392,14 +458,11 @@
     rounds = lax.axis_size("dom").bit_length() - 1
     bound = send_leaf.shape[3]
     received = rounds * bound
-    chunks = -(-kernels // CHUNK)
-    padded = chunks * CHUNK
+    padded = CHUNKS * CHUNK
     half = channels // CORES
-    wide = max(nx, NY)
-    band = half // min(nx, NY)
-    tile = band // (wide // 2)
-    width = channels // 2
-    copies = copy_counts(nx, nz, kernels, rounds)
+    wide, narrow = max(nx, NY), min(nx, NY)
+    band, tile = channels // narrow, channels // (nx * NY)
+    copies = copy_counts(nx, nz, rounds)
     vmem, hbm = (pl.BlockSpec(memory_space=space) for space in (pltpu.VMEM, pltpu.HBM))
     cube = (kernels, channels, channels)
     leaf_shape = (leaves, points, channels)
@@ -437,13 +500,14 @@
             pltpu.VMEM((kernels, leaves * points, channels), BF16),
             pltpu.VMEM((kernels, leaves * points, half), BF16),
             pltpu.VMEM((kernels, half, channels), BF16),
+            pltpu.VMEM((kernels, half // narrow, channels), BF16),
             pltpu.VMEM((wide - 1, kernels, band, channels), BF16),
             pltpu.VMEM((kernels, band, channels), BF16),
-            pltpu.VMEM((wide - 1, kernels, tile, width), BF16),
-            pltpu.VMEM((padded, tile, width), BF16),
-            pltpu.VMEM((chunks, nz - 1, CHUNK // nz, tile, width), BF16),
-            pltpu.VMEM((chunks, CHUNK // nz, tile, width), BF16),
-            pltpu.VMEM((padded, tile, width), BF16),
+            pltpu.VMEM((wide - 1, kernels, tile, channels), BF16),
+            pltpu.VMEM((padded, tile, channels), BF16),
+            pltpu.VMEM((CHUNKS, nz - 1, CHUNK // nz, tile, channels), BF16),
+            pltpu.VMEM((CHUNKS, CHUNK // nz, tile, channels), BF16),
+            pltpu.VMEM((padded, tile, channels), BF16),
             pltpu.VMEM((kernels, band, channels), BF16),
             pltpu.SemaphoreType.DMA((8,)),
             pltpu.SemaphoreType.DMA((copies,)),

time: 57.4 us -> 55.4 us (0.965)
  Pallas kernels: 56.7 us -> 54.7 us
    pallas_call x1, Pallas kernels: 54.5 us -> 52.5 us  [shards(): pl.pallas_call(functools.partial(kernel, nx, nz, kernels, rounds), out_sh...]
where the time goes in v4:
time: 55.4 us; the launch traced here: 55.3 us
  Pallas kernels  54.7 us (99%)
  between operations  0.64 us (1%)
    pallas_call x1, Pallas kernels, shards(): pl.pallas_call(functools.partial(kernel, nx, nz, kernels, rounds), out_sh...  52.5 us
    pallas_call x1, Pallas kernels, shards(): pl.pallas_call(write_kernel, out_shape=(jax.ShapeDtypeStruct(leaf_shape,...  2.14 us

profile of v4, /device:TPU:1, one launch (start us, length us, event | category | flops | bytes accessed | tf_op | source)
XLA Modules:
  0.0 55.3 jit_solution(12796222030687658469)
XLA Ops:
  0.6 52.5 %convolution.1 = (bf16[4,64,256]{2,1,0:T(8,128)(2,1)S(1)}, bf16[4,64,256]{2,1,0:T(8,128)(2,1)S(1)}, bf16[15,256,256]{2,1,0:T(8,128)(2,1)S(1)}) custom-call(bf16[4,64,256]{2,1,0:T(8,128)(2,1)} %bitcast.15, s32[3,1,256]{2,1,0:T(1,128)} %bitcast.17, f32[3,15]{1,0:T(4,128)} %bitcast.18, bf16[15,256,256]{2,1,0:T(8,128)(2,1)} %bitcast.13, s32[4,4]{1,0:T(4,128)} %bitcast.19, ...), custom_call_target="tpu_custom_call" | custom-call | tf_op jit(solution)/shard_map/convolution/pallas_call | solution.py:469
  53.2 2.1 %write.1 = (bf16[4,64,256]{2,1,0:T(8,128)(2,1)}, bf16[4,64,256]{2,1,0:T(8,128)(2,1)}, f32[15,256,256]{2,1,0:T(8,128)}) custom-call(bf16[4,64,256]{2,1,0:T(8,128)(2,1)S(1)} %get-tuple-element.9.output, bf16[4,64,256]{2,1,0:T(8,128)(2,1)S(1)} %get-tuple-element.10.grad, bf16[15,256,256]{2,1,0:T(8,128)(2,1)S(1)} %get-tuple-element.11.mean), custom_call_target="tpu_custom_call" | custom-call | tf_op jit(solution)/shard_map/write/pallas_call | solution.py:529

commit v5 on v4

--- a/solution.py
+++ b/solution.py
@@ -48,8 +48,8 @@
     return lax.dot_general(left, right, (dims, ((), ())), preferred_element_type=F32)
 
 
-def copy_counts(nx, nz, rounds):
-    return 3 * rounds + 1 + CHUNKS * (2 + 6 * (nx - 1 + NY - 1) + 4 + 2 * (nz - 1) + nx + NY)
+def batches(nx):
+    return 5 + 2 * CHUNKS * (5 + nx + 1) + 2 * CHUNKS
 
 
 def kernel(
@@ -102,33 +102,25 @@
         loads[name].start()
 
     number = [0]
-    started = []
-    settled = [0]
-
-    def describe(src, dst, other):
-        index = number[0]
+
+    def batch():
         number[0] += 1
+        return number[0] - 1
+
+    def describe(index, src, dst, other):
         return pltpu.make_async_remote_copy(
             src_ref=src, dst_ref=dst, send_sem=send_sem.at[index], recv_sem=recv_sem.at[index],
             device_id=other, device_id_type=MESH,
         )
 
-    def push(src, dst, other):
-        return begin(describe(src, dst, other))
-
-    def begin(copy):
-        copy.start()
-        started.append(copy)
-        return copy
-
-    def arrive(copies):
-        for copy in copies:
-            copy.wait_recv()
-
-    def settle(count):
-        for copy in started[settled[0] : count]:
-            copy.wait_send()
-        settled[0] = max(settled[0], count)
+    def push(index, src, dst, other):
+        describe(index, src, dst, other).start()
+
+    def arrived(index, like):
+        pltpu.make_async_copy(like, like, recv_sem.at[index]).wait()
+
+    def departed(index, like):
+        pltpu.make_async_copy(like, like, send_sem.at[index]).wait()
 
     for name in ("sends", "coords", "feats"):
         loads[name].wait()
@@ -153,15 +145,17 @@
     def _():
         all_here(1 + len(partners) + len(plane))
 
-    copies_pos, copies_feats = [], []
+    batch_pos, batch_feats, batch_cot, batch_far, batch_near = (batch() for _ in range(5))
     for bit in reversed(range(rounds)):
         entry, there = pl.ds(bit * bound, bound), pl.ds(leaves + bit * bound, bound)
-        copies_pos.append(push(send_pos.at[entry], pool_pos.at[there], partners[bit]))
+        push(batch_pos, send_pos.at[entry], pool_pos.at[there], partners[bit])
     for bit in reversed(range(rounds)):
         entry, there = pl.ds(bit * bound, bound), pl.ds(leaves + bit * bound, bound)
-        copies_feats.append(push(send_feats.at[entry], pool_feats.at[there], partners[bit]))
+        push(batch_feats, send_feats.at[entry], pool_feats.at[there], partners[bit])
+    received = pl.ds(leaves, rounds * bound)
     loads["cot"].wait()
-    copy_cot = push(cot, cot_pair, sibling)
+    copy_cot = describe(batch_cot, cot, cot_pair, sibling)
+    copy_cot.start()
 
     rows = lax.broadcasted_iota(jnp.int32, (points, 2 * points), 0)
     lanes = lax.broadcasted_iota(jnp.int32, (points, 2 * points), 1)
@@ -179,7 +173,7 @@
 
     for name in ("slots", "points", "mask"):
         loads[name].wait()
-    arrive(copies_pos)
+    arrived(batch_pos, pool_pos.at[received])
 
     def correlate(leaf, _):
         for pair in range(near // 2):
@@ -204,7 +198,7 @@
     half = channels // CORES
     own_half = pl.ds(pl.multiple_of(core * half, half), half)
     pair_half = pl.ds(pl.multiple_of((1 - core) * half, half), half)
-    chunks = [(kernels * i // CHUNKS, kernels * (i + 1) // CHUNKS - kernels * i // CHUNKS) for i in range(CHUNKS)]
+    chunks = [(k0, min(CHUNK, kernels - k0)) for k0 in range(0, kernels, CHUNK)]
     groups = []
     for k0, nk in chunks:
         cut = (nk + 1) // 2
@@ -219,45 +213,54 @@
         block = part.shape[1] // axes[axis][1]
         return pl.ds(pl.multiple_of(at * block, block), block)
 
-    firsts, fronts, lasts = {}, {}, {}
+    halves, firsts, owns, fronts, back_own, lasts = ({} for _ in range(6))
+    batch_first, batch_second, batch_back, batch_front, batch_last = ({} for _ in range(5))
     for g0, ng, first, _ in pairs:
         there = pl.ds(g0, ng)
         at, count, to = axes[first]
         block = half // count
-        for side in range(CORES):
-            rows = pl.ds(side * block, block)
-            for step, o in zip(steps_of(count), around(at, count)):
+        halves[g0] = describe(batch(), summed.at[there, :, pair_half], summed_pair.at[there], sibling)
+        for table in (batch_first, batch_second, batch_back, batch_last):
+            table[g0] = batch()
+        for step, o in zip(steps_of(count), around(at, count)):
+            batch_front[g0, step] = batch()
+            for side in range(CORES):
+                rows = pl.ds(side * block, block)
                 firsts[g0, step, side] = describe(
-                    partial.at[there, band(first, o), :], got_first.at[step - 1, there, rows, :], to(o, 1)
+                    batch_first[g0], partial.at[there, band(first, o), :], got_first.at[step - 1, there, rows, :],
+                    to(o, 1),
                 )
                 fronts[g0, step, side] = describe(
-                    gather_second.at[there, rows, :], final.at[there, band(first, at, side * half), :], to(o, side)
+                    batch_front[g0, step], gather_second.at[there, rows, :],
+                    final.at[there, band(first, at, side * half), :], to(o, side),
                 )
-        firsts[g0, 0, 0] = describe(partial.at[there, band(first, at), :], partial_pair.at[there], sibling)
-        fronts[g0, 0, 0] = describe(
-            gather_second.at[there, pl.ds(0, block), :], final.at[there, band(first, at), :], sibling
+        owns[g0] = describe(batch(), partial.at[there, band(first, at), :], partial_pair.at[there], sibling)
+        back_own[g0] = describe(
+            batch(), gather_second.at[there, pl.ds(0, block), :], final.at[there, band(first, at), :], sibling
         )
         for step in range(count):
             here = final.at[there, band(first, lax.rem(at + count - step, count), core * half), :]
-            lasts[g0, step] = describe(here, here, sibling)
-
-    arrive(copies_feats)
+            lasts[g0, step] = describe(batch_last[g0], here, here, sibling)
+    batch_z, batch_back_z = ([batch() for _ in chunks] for _ in range(2))
+
+    def bands(g0, ng, first, count):
+        return final.at[pl.ds(g0, ng), pl.ds(0, count * (half // axes[first][1])), :]
+
+    arrived(batch_feats, pool_feats.at[received])
     for leaf in range(leaves):
         for n in range(near):
             support[leaf, n * points : (n + 1) * points, :] = pool_feats[slots[leaf, n]]
-    copies_summed = []
     for g0, ng, _, _ in pairs:
         for leaf in range(leaves):
             left = h[leaf, g0 : g0 + ng].reshape(ng * points, near * points)
             block = product(left, support[leaf], ((1,), (0,))).astype(BF16)
             summed[g0 : g0 + ng, leaf * points : (leaf + 1) * points, :] = block.reshape(ng, points, channels)
-        there = pl.ds(g0, ng)
-        copies_summed.append(push(summed.at[there, :, pair_half], summed_pair.at[there], sibling))
-
-    arrive([copy_cot])
+        halves[g0].start()
+
+    copy_cot.wait_recv()
     upstream_pair = cot_pair[...].reshape(leaves * points, channels)
-    for copy, (g0, ng, first, _) in zip(copies_summed, pairs):
-        arrive([copy])
+    for g0, ng, first, _ in pairs:
+        halves[g0].wait_recv()
         for k in range(g0, g0 + ng):
             block = product(summed[k, :, own_half].T, upstream, ((1,), (0,)))
             block += product(summed_pair[k].T, upstream_pair, ((1,), (0,)))
@@ -266,8 +269,10 @@
 
             @pl.when(core == side)
             def _():
-                for step in steps_of(axes[first][1]) + [0] * (1 - side):
+                for step in steps_of(axes[first][1]):
                     firsts[g0, step, side].start()
+                if side == 0:
+                    owns[g0].start()
 
     def gathered(entry, total):
         for leaf in range(leaves):
@@ -287,12 +292,28 @@
             grad_support[leaf] = product(left, right, ((0,), (0,)))
         lax.fori_loop(0, rounds * bound, away, 0)
 
-    def hand_back(bits):
-        copies = []
+    def hand_back(index, bits):
         for bit in reversed(bits):
             entry = pl.ds(bit * bound, bound)
-            copies.append(push(send_grad.at[entry], got_grad.at[entry], partners[bit]))
-        return copies
+            push(index, send_grad.at[entry], got_grad.at[entry], partners[bit])
+
+    far, near_by = pl.ds(low * bound, (rounds - low) * bound), pl.ds(0, low * bound)
+
+    def handed_back():
+        arrived(batch_far, got_grad.at[far])
+        arrived(batch_near, got_grad.at[near_by])
+        lax.fori_loop(0, leaves, owned, 0)
+        departed(batch_far, send_grad.at[far])
+        departed(batch_near, send_grad.at[near_by])
+        departed(batch_pos, send_pos)
+        departed(batch_feats, send_feats)
+        copy_cot.wait_send()
+        for copy in halves.values():
+            copy.wait_send()
+
+    def first_left():
+        for g0, ng, first, _ in pairs:
+            departed(batch_first[g0], bands(g0, ng, first, axes[first][1] - 1))
 
     def outputs():
         total = product(summed[0], weights[0], ((1,), (0,)))
@@ -309,51 +330,42 @@
         grad[leaf] = total.astype(BF16)
         return 0
 
-    common = len(started), number[0]
-
     def exchange(side):
         for g0, ng, first, _ in pairs:
             for step in steps_of(axes[first][1])[::-1]:
                 fronts[g0, step, side].wait_recv()
                 lasts[g0, step].start()
             if side == 0:
-                fronts[g0, 0, 0].wait_recv()
-        for (_, step), copy in lasts.items():
-            if step > 0 or side == 0:
-                copy.wait_recv()
-        for (_, step), copy in lasts.items():
-            if step > 0 or side == 1:
-                copy.wait_send()
+                back_own[g0].wait_recv()
+        for g0, ng, first, _ in pairs:
+            count = axes[first][1]
+            arrived(batch_last[g0], bands(g0, ng, first, count - side))
+            departed(batch_last[g0], bands(g0, ng, first, count - 1 + side))
 
     @pl.when(core == 0)
     def _():
         feature_gradients()
-        copies = hand_back(range(rounds))
+        hand_back(batch_far, range(low, rounds))
         outputs()
-        arrive(copies)
-        lax.fori_loop(0, leaves, owned, 0)
-        settle(len(started))
-        for (_, _, side), copy in firsts.items():
-            if side == 0:
-                copy.wait_send()
+        first_left()
+        hand_back(batch_near, range(low))
+        handed_back()
+        for copy in owns.values():
+            copy.wait_send()
         exchange(0)
-
-    del started[common[0] :]
-    number[0], settled[0] = common[1], 0
 
     @pl.when(core == 1)
     def _():
         feature_gradients()
-        copies_grad = hand_back(range(low, rounds))
+        hand_back(batch_far, range(low, rounds))
         outputs()
 
-        seconds = {}
         for g0, ng, first, second in pairs:
             at, count, _ = axes[first]
             block = half // count
-            for step in [0] + steps_of(count)[::-1]:
-                for side in range(CORES if step else 1):
-                    firsts[g0, step, side].wait_recv()
+            there = pl.ds(g0, ng)
+            owns[g0].wait_recv()
+            arrived(batch_first[g0], got_first.at[:, there])
             for k in range(g0, g0 + ng):
                 for side, own in ((0, partial_pair[k]), (1, partial[k, band(first, at), :])):
                     rows = slice(side * block, (side + 1) * block)
@@ -362,22 +374,17 @@
                         total = total + got_first[step, k, rows, :].astype(F32)
                     part[k, rows, :] = total.astype(BF16)
             at, count, to = axes[second]
-            there = pl.ds(g0, ng)
-            seconds[g0] = [
-                push(part.at[there, tile(second, o), :], got_second.at[step, there], to(o, 1))
-                for step, o in enumerate(around(at, count))
-            ]
-        copies_grad += hand_back(range(low))
+            for step, o in enumerate(around(at, count)):
+                push(batch_second[g0], part.at[there, tile(second, o), :], got_second.at[step, there], to(o, 1))
+        hand_back(batch_near, range(low))
 
         per_z = CHUNK // nz
-        early = len(started)
-        thirds = []
         for index, (k0, nk) in enumerate(chunks):
             base = index * CHUNK - k0
             for k in range(k0 + nk, k0 + CHUNK):
                 slab[base + k] = jnp.zeros(slab.shape[1:], BF16)
             for g0, ng, _, second in groups[index]:
-                arrive(seconds[g0])
+                arrived(batch_second[g0], got_second.at[:, pl.ds(g0, ng)])
                 at, count, _ = axes[second]
                 for k in range(g0, g0 + ng):
                     total = part[k, tile(second, at), :].astype(F32)
@@ -385,56 +392,57 @@
                         total = total + got_second[step, k].astype(F32)
                     slab[base + k] = total.astype(BF16)
             at, count, to = axes["z"]
-            thirds.append([
-                push(slab.at[pl.ds(index * CHUNK + o * per_z, per_z)], got_z.at[index, step], to(o, 1))
-                for step, o in enumerate(around(at, count))
-            ])
+            for step, o in enumerate(around(at, count)):
+                push(batch_z[index], slab.at[pl.ds(index * CHUNK + o * per_z, per_z)], got_z.at[index, step], to(o, 1))
         devices = nx * NY * nz * CORES
-        back_z = []
-        for index, copies in enumerate(thirds):
-            arrive(copies)
+        for index in range(CHUNKS):
+            arrived(batch_z[index], got_z.at[index])
             at, count, to = axes["z"]
             own = pl.ds(index * CHUNK + z * per_z, per_z)
             total = slab[own].astype(F32)
             for step in range(count - 1):
                 total = total + got_z[index, step].astype(F32)
             piece[index] = (total / devices).astype(BF16)
-            back_z.append([push(piece.at[index], gather_z.at[own], to(o, 1)) for o in around(at, count)])
+            for o in around(at, count):
+                push(batch_back_z[index], piece.at[index], gather_z.at[own], to(o, 1))
             gather_z[own] = piece[index]
-        arrive(copies_grad)
-        lax.fori_loop(0, leaves, owned, 0)
-        settle(early)
-
-        back_second = {}
+
+        handed_back()
+        first_left()
+
         for index, (k0, nk) in enumerate(chunks):
-            arrive(back_z[index])
+            arrived(batch_back_z[index], got_z.at[index])
             for g0, ng, _, second in groups[index]:
                 at, count, to = axes[second]
                 there, here = pl.ds(g0, ng), pl.ds(index * CHUNK + g0 - k0, ng)
                 own = tile(second, at)
-                back_second[g0] = [
-                    push(gather_z.at[here], gather_second.at[there, own, :], to(o, 1)) for o in around(at, count)
-                ]
+                for o in around(at, count):
+                    push(batch_back[g0], gather_z.at[here], gather_second.at[there, own, :], to(o, 1))
                 gather_second[there, own, :] = gather_z[here]
         for g0, ng, first, _ in pairs:
-            arrive(back_second[g0])
+            there = pl.ds(g0, ng)
+            arrived(batch_back[g0], got_second.at[:, there])
             at, count, _ = axes[first]
             block = half // count
-            for step in steps_of(count) + [0]:
-                for side in range(CORES if step else 1):
+            for step in steps_of(count):
+                for side in range(CORES):
                     fronts[g0, step, side].start()
-            there = pl.ds(g0, ng)
+            back_own[g0].start()
             for side in range(CORES):
                 rows = slice(side * block, (side + 1) * block)
                 final[there, band(first, at, side * half), :] = gather_second[there, rows, :]
             lasts[g0, 0].start()
-        settle(len(started))
-        for (_, _, side), copy in firsts.items():
-            if side == 1:
-                copy.wait_send()
+        for index in range(CHUNKS):
+            departed(batch_z[index], got_z.at[index])
+            departed(batch_back_z[index], got_z.at[index])
+        for g0, ng, _, _ in pairs:
+            departed(batch_second[g0], got_second.at[:, pl.ds(g0, ng)])
+            departed(batch_back[g0], got_second.at[:, pl.ds(g0, ng)])
         exchange(1)
-        for copy in fronts.values():
-            copy.wait_send()
+        for g0, ng, first, _ in pairs:
+            back_own[g0].wait_send()
+            for step in steps_of(axes[first][1]):
+                departed(batch_front[g0, step], gather_second.at[pl.ds(g0, ng)])
 
 
 def write_kernel(output, grad, mean, output_out, grad_out, mean_out, wide, sem):
@@ -462,7 +470,7 @@
     half = channels // CORES
     wide, narrow = max(nx, NY), min(nx, NY)
     band, tile = channels // narrow, channels // (nx * NY)
-    copies = copy_counts(nx, nz, rounds)
+    copies = batches(max(nx, NY))
     vmem, hbm = (pl.BlockSpec(memory_space=space) for space in (pltpu.VMEM, pltpu.HBM))
     cube = (kernels, channels, channels)
     leaf_shape = (leaves, points, channels)

time: 55.4 us -> 53.6 us (0.968)
  Pallas kernels: 54.7 us -> 52.8 us
    pallas_call x1, Pallas kernels: 52.5 us -> 50.7 us  [shards(): pl.pallas_call(functools.partial(kernel, nx, nz, kernels, rounds), out_sh...]
where the time goes in v5:
time: 53.6 us; the launch traced here: 53.5 us
  Pallas kernels  52.8 us (99%)
  between operations  0.64 us (1%)
    pallas_call x1, Pallas kernels, shards(): pl.pallas_call(functools.partial(kernel, nx, nz, kernels, rounds), out_sh...  50.7 us
    pallas_call x1, Pallas kernels, shards(): pl.pallas_call(write_kernel, out_shape=(jax.ShapeDtypeStruct(leaf_shape,...  2.14 us

profile of v5, /device:TPU:1, one launch (start us, length us, event | category | flops | bytes accessed | tf_op | source)
XLA Modules:
  0.0 53.5 jit_solution(15771909088472836799)
XLA Ops:
  0.6 50.7 %convolution.1 = (bf16[4,64,256]{2,1,0:T(8,128)(2,1)S(1)}, bf16[4,64,256]{2,1,0:T(8,128)(2,1)S(1)}, bf16[15,256,256]{2,1,0:T(8,128)(2,1)S(1)}) custom-call(bf16[4,64,256]{2,1,0:T(8,128)(2,1)} %bitcast.15, s32[3,1,256]{2,1,0:T(1,128)} %bitcast.17, f32[3,15]{1,0:T(4,128)} %bitcast.18, bf16[15,256,256]{2,1,0:T(8,128)(2,1)} %bitcast.13, s32[4,4]{1,0:T(4,128)} %bitcast.19, ...), custom_call_target="tpu_custom_call" | custom-call | tf_op jit(solution)/shard_map/convolution/pallas_call | solution.py:477
  51.3 2.1 %write.1 = (bf16[4,64,256]{2,1,0:T(8,128)(2,1)}, bf16[4,64,256]{2,1,0:T(8,128)(2,1)}, f32[15,256,256]{2,1,0:T(8,128)}) custom-call(bf16[4,64,256]{2,1,0:T(8,128)(2,1)S(1)} %get-tuple-element.9.output, bf16[4,64,256]{2,1,0:T(8,128)(2,1)S(1)} %get-tuple-element.10.grad, bf16[15,256,256]{2,1,0:T(8,128)(2,1)S(1)} %get-tuple-element.11.mean), custom_call_target="tpu_custom_call" | custom-call | tf_op jit(solution)/shard_map/write/pallas_call | solution.py:537

commit v6 on v5

--- a/solution.py
+++ b/solution.py
@@ -86,11 +86,11 @@
 
     @pl.when(core == 1)
     def _():
-        greet([sibling] + [to(o, 1) for to, o in plane + rings["z"]] + [to(o, 0) for to, o in plane])
+        greet([to(o, 1) for to, o in rings["z"] + plane] + [to(o, 0) for to, o in plane] + [sibling])
 
     @pl.when(core == 0)
     def _():
-        greet([sibling] + partners + [to(o, 1) for to, o in plane])
+        greet(partners[::-1] + [to(o, 1) for to, o in plane] + [sibling])
 
     loads = {}
     for index, (name, src, dst) in enumerate((
@@ -99,6 +99,8 @@
         ("weights", weights_in, weights), ("mask", mask_in, mask),
     )):
         loads[name] = pltpu.make_async_copy(src, dst, local_sem.at[index])
+    early = ("sends", "coords", "feats")
+    for name in early:
         loads[name].start()
 
     number = [0]
@@ -122,8 +124,11 @@
     def departed(index, like):
         pltpu.make_async_copy(like, like, send_sem.at[index]).wait()
 
-    for name in ("sends", "coords", "feats"):
+    for name in early:
         loads[name].wait()
+    for name in loads:
+        if name not in early:
+            loads[name].start()
     positions = coords[...].reshape(3, leaves * points).astype(F32) * QUANT
     for leaf in range(leaves):
         own = positions[:, leaf * points : (leaf + 1) * points]
@@ -202,7 +207,10 @@
     groups = []
     for k0, nk in chunks:
         cut = (nk + 1) // 2
-        groups.append([(k0, cut, "x", "y"), (k0 + cut, nk - cut, "y", "x")])
+        if k0 == 0:
+            groups.append([(k0, cut, "x", "y"), (k0 + cut, nk - cut, "y", "x")])
+        else:
+            groups.append([(k0, nk - cut, "y", "x"), (k0 + nk - cut, cut, "x", "y")])
     pairs = sum(groups, [])
 
     def band(axis, at, start=0):
@@ -339,14 +347,20 @@
                 back_own[g0].wait_recv()
         for g0, ng, first, _ in pairs:
             count = axes[first][1]
-            arrived(batch_last[g0], bands(g0, ng, first, count - side))
+            if side == 1:
+                back_own[g0].wait_send()
+                for step in steps_of(count):
+                    departed(batch_front[g0, step], gather_second.at[pl.ds(g0, ng)])
             departed(batch_last[g0], bands(g0, ng, first, count - 1 + side))
+        for g0, ng, first, _ in pairs:
+            arrived(batch_last[g0], bands(g0, ng, first, axes[first][1] - side))
+
+    feature_gradients()
+    hand_back(batch_far, range(low, rounds))
+    outputs()
 
     @pl.when(core == 0)
     def _():
-        feature_gradients()
-        hand_back(batch_far, range(low, rounds))
-        outputs()
         first_left()
         hand_back(batch_near, range(low))
         handed_back()
@@ -356,10 +370,6 @@
 
     @pl.when(core == 1)
     def _():
-        feature_gradients()
-        hand_back(batch_far, range(low, rounds))
-        outputs()
-
         for g0, ng, first, second in pairs:
             at, count, _ = axes[first]
             block = half // count
@@ -431,6 +441,7 @@
             for side in range(CORES):
                 rows = slice(side * block, (side + 1) * block)
                 final[there, band(first, at, side * half), :] = gather_second[there, rows, :]
+        for g0, _, _, _ in pairs:
             lasts[g0, 0].start()
         for index in range(CHUNKS):
             departed(batch_z[index], got_z.at[index])
@@ -439,10 +450,6 @@
             departed(batch_second[g0], got_second.at[:, pl.ds(g0, ng)])
             departed(batch_back[g0], got_second.at[:, pl.ds(g0, ng)])
         exchange(1)
-        for g0, ng, first, _ in pairs:
-            back_own[g0].wait_send()
-            for step in steps_of(axes[first][1]):
-                departed(batch_front[g0, step], gather_second.at[pl.ds(g0, ng)])
 
 
 def write_kernel(output, grad, mean, output_out, grad_out, mean_out, wide, sem):

time: 53.6 us -> 53.2 us (level)
  no operation moved by 1% of the time
where the time goes in v6:
time: 53.2 us; the launch traced here: 53 us
  Pallas kernels  52.3 us (98%)
  between operations  0.64 us (1%)
    pallas_call x1, Pallas kernels, shards(): pl.pallas_call(functools.partial(kernel, nx, nz, kernels, rounds), out_sh...  50.2 us
    pallas_call x1, Pallas kernels, shards(): pl.pallas_call(write_kernel, out_shape=(jax.ShapeDtypeStruct(leaf_shape,...  2.14 us

profile of v6, /device:TPU:1, one launch (start us, length us, event | category | flops | bytes accessed | tf_op | source)
XLA Modules:
  0.0 53.0 jit_solution(13010530517691083737)
XLA Ops:
  0.6 50.2 %convolution.1 = (bf16[4,64,256]{2,1,0:T(8,128)(2,1)S(1)}, bf16[4,64,256]{2,1,0:T(8,128)(2,1)S(1)}, bf16[15,256,256]{2,1,0:T(8,128)(2,1)S(1)}) custom-call(bf16[4,64,256]{2,1,0:T(8,128)(2,1)} %bitcast.15, s32[3,1,256]{2,1,0:T(1,128)} %bitcast.17, f32[3,15]{1,0:T(4,128)} %bitcast.18, bf16[15,256,256]{2,1,0:T(8,128)(2,1)} %bitcast.13, s32[4,4]{1,0:T(4,128)} %bitcast.19, ...), custom_call_target="tpu_custom_call" | custom-call | tf_op jit(solution)/shard_map/convolution/pallas_call | solution.py:484
  50.8 2.1 %write.1 = (bf16[4,64,256]{2,1,0:T(8,128)(2,1)}, bf16[4,64,256]{2,1,0:T(8,128)(2,1)}, f32[15,256,256]{2,1,0:T(8,128)}) custom-call(bf16[4,64,256]{2,1,0:T(8,128)(2,1)S(1)} %get-tuple-element.9.output, bf16[4,64,256]{2,1,0:T(8,128)(2,1)S(1)} %get-tuple-element.10.grad, bf16[15,256,256]{2,1,0:T(8,128)(2,1)S(1)} %get-tuple-element.11.mean), custom_call_target="tpu_custom_call" | custom-call | tf_op jit(solution)/shard_map/write/pallas_call | solution.py:544

commit v7 on v6

--- a/solution.py
+++ b/solution.py
@@ -49,7 +49,7 @@
 
 
 def batches(nx):
-    return 5 + 2 * CHUNKS * (5 + nx + 1) + 2 * CHUNKS
+    return 5 + 2 * CHUNKS * 8 + 2 * CHUNKS
 
 
 def kernel(
@@ -222,16 +222,15 @@
         return pl.ds(pl.multiple_of(at * block, block), block)
 
     halves, firsts, owns, fronts, back_own, lasts = ({} for _ in range(6))
-    batch_first, batch_second, batch_back, batch_front, batch_last = ({} for _ in range(5))
+    batch_first, batch_second, batch_back, batch_front = ({} for _ in range(4))
     for g0, ng, first, _ in pairs:
         there = pl.ds(g0, ng)
         at, count, to = axes[first]
         block = half // count
         halves[g0] = describe(batch(), summed.at[there, :, pair_half], summed_pair.at[there], sibling)
-        for table in (batch_first, batch_second, batch_back, batch_last):
+        for table in (batch_first, batch_second, batch_back, batch_front):
             table[g0] = batch()
         for step, o in zip(steps_of(count), around(at, count)):
-            batch_front[g0, step] = batch()
             for side in range(CORES):
                 rows = pl.ds(side * block, block)
                 firsts[g0, step, side] = describe(
@@ -239,16 +238,15 @@
                     to(o, 1),
                 )
                 fronts[g0, step, side] = describe(
-                    batch_front[g0, step], gather_second.at[there, rows, :],
+                    batch_front[g0], gather_second.at[there, rows, :],
                     final.at[there, band(first, at, side * half), :], to(o, side),
                 )
         owns[g0] = describe(batch(), partial.at[there, band(first, at), :], partial_pair.at[there], sibling)
         back_own[g0] = describe(
             batch(), gather_second.at[there, pl.ds(0, block), :], final.at[there, band(first, at), :], sibling
         )
-        for step in range(count):
-            here = final.at[there, band(first, lax.rem(at + count - step, count), core * half), :]
-            lasts[g0, step] = describe(batch_last[g0], here, here, sibling)
+        here = final.at[there, own_half, :]
+        lasts[g0] = describe(batch(), here, here, sibling)
     batch_z, batch_back_z = ([batch() for _ in chunks] for _ in range(2))
 
     def bands(g0, ng, first, count):
@@ -340,20 +338,19 @@
 
     def exchange(side):
         for g0, ng, first, _ in pairs:
-            for step in steps_of(axes[first][1])[::-1]:
-                fronts[g0, step, side].wait_recv()
-                lasts[g0, step].start()
+            count = axes[first][1]
+            arrived(batch_front[g0], bands(g0, ng, first, count - 1))
             if side == 0:
                 back_own[g0].wait_recv()
+            lasts[g0].start()
         for g0, ng, first, _ in pairs:
             count = axes[first][1]
             if side == 1:
                 back_own[g0].wait_send()
-                for step in steps_of(count):
-                    departed(batch_front[g0, step], gather_second.at[pl.ds(g0, ng)])
-            departed(batch_last[g0], bands(g0, ng, first, count - 1 + side))
-        for g0, ng, first, _ in pairs:
-            arrived(batch_last[g0], bands(g0, ng, first, axes[first][1] - side))
+                departed(batch_front[g0], bands(g0, ng, first, CORES * (count - 1)))
+            lasts[g0].wait_send()
+        for copy in lasts.values():
+            copy.wait_recv()
 
     feature_gradients()
     hand_back(batch_far, range(low, rounds))
@@ -438,11 +435,7 @@
                 for side in range(CORES):
                     fronts[g0, step, side].start()
             back_own[g0].start()
-            for side in range(CORES):
-                rows = slice(side * block, (side + 1) * block)
-                final[there, band(first, at, side * half), :] = gather_second[there, rows, :]
-        for g0, _, _, _ in pairs:
-            lasts[g0, 0].start()
+            final[there, band(first, at, half), :] = gather_second[there, block : CORES * block, :]
         for index in range(CHUNKS):
             departed(batch_z[index], got_z.at[index])
             departed(batch_back_z[index], got_z.at[index])

time: 53.2 us -> 53.1 us (level)
  no operation moved by 1% of the time
where the time goes in v7:
time: 53.1 us; the launch traced here: 53 us
  Pallas kernels  52.3 us (98%)
  between operations  0.64 us (1%)
    pallas_call x1, Pallas kernels, shards(): pl.pallas_call(functools.partial(kernel, nx, nz, kernels, rounds), out_sh...  50.2 us
    pallas_call x1, Pallas kernels, shards(): pl.pallas_call(write_kernel, out_shape=(jax.ShapeDtypeStruct(leaf_shape,...  2.14 us

profile of v7, /device:TPU:1, one launch (start us, length us, event | category | flops | bytes accessed | tf_op | source)
XLA Modules:
  0.0 53.0 jit_solution(2871724501868953953)
XLA Ops:
  0.6 50.2 %convolution.1 = (bf16[4,64,256]{2,1,0:T(8,128)(2,1)S(1)}, bf16[4,64,256]{2,1,0:T(8,128)(2,1)S(1)}, bf16[15,256,256]{2,1,0:T(8,128)(2,1)S(1)}) custom-call(bf16[4,64,256]{2,1,0:T(8,128)(2,1)} %bitcast.15, s32[3,1,256]{2,1,0:T(1,128)} %bitcast.17, f32[3,15]{1,0:T(4,128)} %bitcast.18, bf16[15,256,256]{2,1,0:T(8,128)(2,1)} %bitcast.13, s32[4,4]{1,0:T(4,128)} %bitcast.19, ...), custom_call_target="tpu_custom_call" | custom-call | tf_op jit(solution)/shard_map/convolution/pallas_call | solution.py:477
  50.8 2.1 %write.1 = (bf16[4,64,256]{2,1,0:T(8,128)(2,1)}, bf16[4,64,256]{2,1,0:T(8,128)(2,1)}, f32[15,256,256]{2,1,0:T(8,128)}) custom-call(bf16[4,64,256]{2,1,0:T(8,128)(2,1)S(1)} %get-tuple-element.9.output, bf16[4,64,256]{2,1,0:T(8,128)(2,1)S(1)} %get-tuple-element.10.grad, bf16[15,256,256]{2,1,0:T(8,128)(2,1)S(1)} %get-tuple-element.11.mean), custom_call_target="tpu_custom_call" | custom-call | tf_op jit(solution)/shard_map/write/pallas_call | solution.py:537
